TPU v7x, 32 devices: a whole 2x2x4 slice. The times are simulated.
32 devices in a mesh: seq: 16 (over z, x, core), cand: 2 (over y).
Axes of the slice: x: 2, y: 2, z: 4, core: 2. Of those that a mesh axis runs over, the one named last changes fastest.
Arguments:
- behaviors: float32 [2, 131072, 128], P('cand', 'seq'), may hold values from -15 to 15
- cluster_ids: int32 [2, 131072], P('cand', 'seq'), may hold values from 0 to 2047, as said below
- lengths: int32 [2, 16], P('cand', 'seq'), may hold values from 2048 to 8192
- candidates: bfloat16 [2, 1024, 128], P(None, ('seq', 'cand')), may hold values from -6 to 6
- w_query: bfloat16 [128, 128], replicated, may hold values from -0.5 to 0.5
- w_key: bfloat16 [128, 128], replicated, may hold values from -0.5 to 0.5
- w_hidden: bfloat16 [256, 512], replicated, may hold values from -0.375 to 0.375
- b_hidden: float32 [512], replicated, may hold values from -0.5 to 0.5
- w_out: float32 [512], replicated, may hold values from -0.25 to 0.25
Outputs:
- ranking: float32 [2, 1024], P(None, ('seq', 'cand'))
Inputs may be any that keep to these rules, and one draw needn't show every extreme that they name: `cluster_ids`: each user's first 2048 slots name 2048 different clusters.
All inputs are finite; a program needn't handle non-finite values.
Results may differ from a plain program's by a relative error of at most 0.02.
Values may be sent and summed in bfloat16 or wider, within the bound.
No kernel may reach another device: no remote copies, remote signals or barrier semaphores. Data moves between devices by JAX's collectives and lax.ppermute only.
A program may use at most 64 MiB of HBM per device.

v0:
```python
import jax
import jax.numpy as jnp
from jax import lax
from jax.sharding import PartitionSpec as P

C = 2048


def cluster_partials(item_rows, cluster_ids, length):
    slots = item_rows.shape[0]
    block_rows = min(512, slots)
    labels = jnp.arange(C, dtype=jnp.int32)

    def accumulate(carry, number):
        totals, tallies = carry
        offset = number * block_rows
        piece = lax.dynamic_slice_in_dim(item_rows, offset, block_rows, 0)
        idents = lax.dynamic_slice_in_dim(cluster_ids, offset, block_rows, 0)
        inside = offset + jnp.arange(block_rows, dtype=jnp.int32) < length
        onehot = ((idents[:, None] == labels[None, :]) & inside[:, None]).astype(jnp.bfloat16)
        upper = lax.optimization_barrier(piece.astype(jnp.bfloat16))
        lower = (piece - upper.astype(jnp.float32)).astype(jnp.bfloat16)
        dims = (((0,), (0,)), ((), ()))
        totals = totals + lax.dot_general(onehot, upper, dims, preferred_element_type=jnp.float32)
        totals = totals + lax.dot_general(onehot, lower, dims, preferred_element_type=jnp.float32)
        tallies = tallies + jnp.sum(onehot, axis=0, dtype=jnp.float32)
        return ((totals, tallies), None)

    start = (jnp.zeros((C, item_rows.shape[1]), jnp.float32), jnp.zeros((C,), jnp.float32))
    (totals, tallies), _ = lax.scan(
        accumulate, start, jnp.arange(slots // block_rows, dtype=jnp.int32)
    )
    return (totals, tallies)


def statistics(sums, counts):
    centroids = (sums / jnp.maximum(counts, 1.0)[..., None]).astype(jnp.bfloat16)
    size_bias = jnp.where(counts > 0, jnp.log(1.0 + counts), jnp.float32(-1000000000.0)).astype(
        jnp.bfloat16
    )
    return (centroids, size_bias)


def make_keys(centroids, w_key):
    return jnp.einsum("ukd,de->uke", centroids, w_key, preferred_element_type=jnp.float32).astype(
        jnp.bfloat16
    )


def rank_rows(candidates, key_rows, centroids, size_bias, w_query, w_hidden, b_hidden, w_out):
    users, local_cands, width = candidates.shape
    queries = jnp.dot(
        candidates.reshape(users * local_cands, width), w_query, preferred_element_type=jnp.float32
    )
    queries = queries.astype(jnp.bfloat16).reshape(users, local_cands, width)
    scores = jnp.einsum(
        "ucd,ukd->uck", queries, key_rows, preferred_element_type=jnp.float32
    ) / jnp.sqrt(jnp.float32(width))
    scores = scores + size_bias.astype(jnp.float32)[:, None, :]
    weights = jax.nn.softmax(scores, axis=-1).astype(jnp.bfloat16)
    attended = jnp.einsum(
        "uck,ukd->ucd", weights, centroids, preferred_element_type=jnp.float32
    ).astype(jnp.bfloat16)
    features = jnp.concatenate([candidates, attended], axis=-1).reshape(
        users * local_cands, 2 * width
    )
    hidden = jax.nn.relu(jnp.dot(features, w_hidden, preferred_element_type=jnp.float32) + b_hidden)
    ranking = jnp.dot(hidden, w_out, precision=lax.Precision.HIGHEST)
    return ranking.reshape(users, local_cands)


def on_device(
    behaviors, cluster_ids, lengths, candidates, w_query, w_key, w_hidden, b_hidden, w_out
):
    partials, counts = jax.vmap(cluster_partials)(behaviors, cluster_ids, lengths[:, 0])
    sums, tallies = (
        lax.psum(partials.astype(jnp.bfloat16), "seq").astype(jnp.float32),
        lax.psum(counts.astype(jnp.bfloat16), "seq").astype(jnp.float32),
    )
    centroids, size_bias = statistics(sums, tallies)
    key_rows = make_keys(centroids, w_key)
    mine = lax.all_to_all(candidates, "cand", split_axis=0, concat_axis=1, tiled=True)
    scored = rank_rows(mine, key_rows, centroids, size_bias, w_query, w_hidden, b_hidden, w_out)
    return lax.all_to_all(scored, "cand", split_axis=1, concat_axis=0, tiled=True)


def solution(mesh):
    in_specs = (
        P("cand", "seq", None),
        P("cand", "seq"),
        P("cand", "seq"),
        P(None, ("seq", "cand"), None),
        P(),
        P(),
        P(),
        P(),
        P(),
    )
    out_specs = P(None, ("seq", "cand"))
    return jax.shard_map(
        on_device, mesh=mesh, in_specs=in_specs, out_specs=out_specs, check_vma=False
    )
```

profile of v0, /device:TPU:0, one launch (start us, length us, event | category | flops | bytes accessed | tf_op | source)
XLA Modules:
  0.0 256.1 jit_solution(15629798256894113474)
XLA Ops:
  6.6 138.9 %while.16 = (s32[]{:T(128)}, f32[1,2048,128]{2,1,0:T(8,128)S(1)}, f32[1,2048]{1,0:T(1,128)S(1)}, s32[16]{0:T(128)S(1)}, s32[1,8192]{1,0:T(1,128)}, /*index=5*/s3...) while((s32[]{:T(128)}, f32[1,2048,128]{2,1,0:T(8,128)S(1)}, ...), condition=%wide.region_2.3_spmd.clone.clone, body=%wide.region_0.2_spmd.clone.clone.sunk | while | flops 547294208 | bytes 5026014 | solution.py:30
  10.4 1.5 fusion.67
  11.9 2.5 fusion.68
  19.1 1.5 fusion.67
  20.6 2.5 fusion.68
  27.8 1.5 fusion.67
  29.3 2.5 fusion.68
  37.9 2.5 fusion.68
  45.1 1.5 fusion.67
  46.6 2.5 fusion.68
  55.3 2.5 fusion.68
  64.0 2.5 fusion.68
  71.2 1.5 fusion.67
  72.7 2.5 fusion.68
  79.9 1.5 fusion.67
  81.3 2.5 fusion.68
  88.5 1.5 fusion.67
  90.0 2.5 fusion.68
  98.7 2.5 fusion.68
  107.4 2.5 fusion.68
  114.6 1.5 fusion.67
  116.1 2.5 fusion.68
  123.3 1.5 fusion.67
  124.7 2.5 fusion.68
  133.4 2.5 fusion.68
  140.6 1.5 fusion.67
  142.1 2.5 fusion.68
  146.3 4.2 %all-to-all-start = ((bf16[2,32,128]{2,1,0:T(8,128)(2,1)}), bf16[2,32,128]{2,1,0:T(8,128)(2,1)S(1)}, u32[]{:S(2)}, u32[]{:S(2)}) async-start(bf16[2,32,128]{2,1,0:T(8,128)(2,1)} %param.14), calls=%async_computation | async-start | bytes 32768 | tf_op jit(solution)/shard_map/all_to_all | solution.py:82
  150.6 34.7 %psum.15 = bf16[1,2048]{1,0:T(2,128)(2,1)S(1)} all-reduce(bf16[1,2048]{1,0:T(2,128)(2,1)S(1)} %convert_element_type.78), channel_id=1, replica_groups=mesh['seq'=16,'cand'=2] {'seq'}, use_global_device_ids=true, to_apply=%region_4.5 | all-reduce | flops 2048 | bytes 8192 | tf_op jit(solution)/shard_map/psum | solution.py:78
  185.5 53.7 %all-reduce.2.cloned.1.call-done = bf16[1,2048,128]{2,1,0:T(8,128)(2,1)} async-done(((bf16[1,2048,128]{2,1,0:T(8,128)(2,1)}), bf16[1,2048,128]{2,1,0:T(8,128)(2,1)}) %all-reduce.2.cloned.1.call-update) | async-done | bytes 524304 | tf_op jit(solution)/shard_map/psum | solution.py:77
  239.3 1.9 fusion.46
  242.4 6.3 %all_to_all.28 = f32[1,2,32]{2,0,1:T(1,128)S(1)} all-to-all(f32[1,2,32]{2,0,1:T(1,128)S(1)} %bitcast.104), channel_id=1, replica_groups=mesh['seq'=16,'cand'=2] {'cand'}, dimensions={1} | all-to-all | bytes 512 | tf_op jit(solution)/shard_map/all_to_all | solution.py:84
  (146 shorter events, 75.6 us)
Async XLA Ops:
  6.5 235.4 %copy-start = (bf16[256,512]{1,0:T(8,128)(2,1)S(1)}, bf16[256,512]{1,0:T(8,128)(2,1)}, u32[]{:S(2)}) copy-start(bf16[256,512]{1,0:T(8,128)(2,1)} %param.17) | copy-start | bytes 786436
  6.5 232.7 %all-reduce.2.cloned.1.call-start = ((), (), s32[]{:S(2)}) async-start(), calls=%async_computation.2 | async-start | bytes 1048576 | tf_op jit(solution)/shard_map/psum | solution.py:77
  6.5 178.8 %copy-start.1 = (bf16[128,128]{1,0:T(8,128)(2,1)S(1)}, bf16[128,128]{1,0:T(8,128)(2,1)}, u32[]{:S(2)}) copy-start(bf16[128,128]{1,0:T(8,128)(2,1)} %param.15) | copy-start | bytes 98308
  6.6 232.7 %copy-start.5 = (bf16[128,128]{1,0:T(8,128)(2,1)S(1)}, bf16[128,128]{1,0:T(8,128)(2,1)}, u32[]{:S(2)}) copy-start(bf16[128,128]{1,0:T(8,128)(2,1)} %param.16) | copy-start | bytes 98308
  146.3 39.0 %all-to-all-start = ((bf16[2,32,128]{2,1,0:T(8,128)(2,1)}), bf16[2,32,128]{2,1,0:T(8,128)(2,1)S(1)}, u32[]{:S(2)}, u32[]{:S(2)}) async-start(bf16[2,32,128]{2,1,0:T(8,128)(2,1)} %param.14), calls=%async_computation | async-start | bytes 32768 | tf_op jit(solution)/shard_map/all_to_all | solution.py:82
  239.3 2.1 copy-start.4
  241.1 0.8 copy-start.2
  241.1 1.0 copy-start.3
Sparse Core Ops, SparseCore 0:
  146.5 92.7 all-reduce.1
where the time goes:
time: 258 us; the launch traced here: 256 us
  matrix products  65.8 us (26%)
  waiting for transfers between devices  53.8 us (21%)
  blocking collectives  41 us (16%)
  local copies, waits for them, and re-layouts  38.8 us (15%)
  other arithmetic  26.9 us (10%)
  between operations  13.5 us (5%)
  loops' own time  12 us (5%)
  starting transfers between devices  4.25 us (2%)
    psum x1, waiting for transfers between devices, on_device(): lax.psum(partials.astype(jnp.bfloat16), 'seq').astype(jnp.float32)  53.7 us
    dot_general x16, matrix products, accumulate(): lax.dot_general(onehot, lower, dims, preferred_element_type=jnp.float32)  39.4 us
    psum x1, blocking collectives, on_device(): lax.psum(counts.astype(jnp.bfloat16), 'seq').astype(jnp.float32)  34.7 us
    dot_general x16, matrix products, accumulate(): lax.dot_general(onehot, upper, dims, preferred_element_type=jnp.float32)  23.6 us
    convert_element_type x16, local copies, waits for them, and re-layouts, accumulate(): upper = lax.optimization_barrier(piece.astype(jnp.bfloat16))  16.5 us
    reduce_sum x16, other arithmetic, accumulate(): tallies = tallies + jnp.sum(onehot, axis=0, dtype=jnp.float32)  13.7 us
    another operation x1, loops' own time, cluster_partials(): lax.scan(accumulate, start, jnp.arange(slots // block_rows, dtype=jnp.int...  12 us
    while x16, local copies, waits for them, and re-layouts, accumulate(): idents = lax.dynamic_slice_in_dim(cluster_ids, offset, block_rows, 0)  11 us
  transfers between devices with their start and end apart: 2, of which 1 were waited for; matrix products, arithmetic and copies ran while one was open for 0% of the time, Pallas kernels for 0%

commit v1 on v0

v1 whole, which is shorter than its diff:
```python
import functools

import jax
import jax.numpy as jnp
from jax import lax
from jax.experimental import pallas as pl
from jax.experimental.pallas import tpu as pltpu
from jax.sharding import PartitionSpec as P

CLUSTERS = 2048
BF = jnp.bfloat16
F32 = jnp.float32
PAD = 16
SHARERS = 4
NT = (((1,), (1,)), ((), ()))
TN = (((0,), (0,)), ((), ()))
NN = (((1,), (0,)), ((), ()))


def digit_plan(parts, slots):
    bits = 1
    while parts * (2 ** (bits + 1) - 1) <= 256:
        bits += 1
    return bits, -(-(slots.bit_length()) // bits)


def pool_kernel(
    width, low, bits, digits, scalars, ids_ref, rows_ref, send_ref, next_ref, mine_ref, total
):
    step, steps = pl.program_id(0), pl.num_programs(0)
    block = rows_ref.shape[0]
    groups = total.shape[0] // width
    turned = jnp.transpose(rows_ref[...]).astype(BF)
    ids = ids_ref[...]
    slot = step * block + lax.broadcasted_iota(jnp.int32, ids.shape, 1)
    shift = low.bit_length() - 1
    high = jnp.where(slot < scalars[0], (ids >> shift) ^ scalars[1], -1)
    high = high.astype(F32).astype(BF)
    within = (ids & (low - 1)).astype(F32).astype(BF)
    labels = lax.broadcasted_iota(jnp.int32, (low, 1), 0).astype(F32).astype(BF)
    onehot = jnp.where(labels == within, BF(1), BF(0))
    pieces = [jnp.where(high == BF(h), turned, BF(0)) for h in range(groups)]
    names = lax.broadcasted_iota(jnp.int32, (PAD, 1), 0).astype(F32).astype(BF)
    pieces.append(jnp.where(names == high, BF(1), BF(0)))
    part = lax.dot_general(
        jnp.concatenate(pieces, 0), onehot, NT, preferred_element_type=F32
    )

    @pl.when(step == 0)
    def _():
        total[...] = part

    @pl.when(step > 0)
    def _():
        total[...] += part

    @pl.when(step == steps - 1)
    def _():
        pairs = groups // 2
        counts = total[groups * width : groups * width + PAD, :].astype(jnp.int32)
        row = lax.broadcasted_iota(jnp.int32, (PAD, 1), 0)

        def block_of(pair):
            tally = jnp.zeros((PAD, low), jnp.int32)
            for k in range(2):
                for d in range(digits):
                    one = (counts[2 * pair + k : 2 * pair + k + 1, :] >> (bits * d)) & (2**bits - 1)
                    tally = jnp.where(row == k * digits + d, one, tally)
            return total[2 * pair * width : 2 * (pair + 1) * width, :], tally.astype(F32)

        for pair in range(pairs):
            sums, tally = block_of(pair)
            if pair == 0:
                dest = mine_ref
            elif pair == 1:
                dest = next_ref
            else:
                dest = send_ref.at[pair - 2]
            dest[: 2 * width, :] = sums.astype(dest.dtype)
            dest[2 * width :, :] = tally.astype(dest.dtype)


def pool(rows, ids, scalars, parts):
    slots, width = rows.shape
    low = CLUSTERS // (2 * SHARERS)
    bits, digits = digit_plan(parts, slots)
    block = min(2048, slots)
    groups = CLUSTERS // low
    height = 2 * width + PAD
    return pl.pallas_call(
        functools.partial(pool_kernel, width, low, bits, digits),
        grid=(slots // block,),
        in_specs=[
            pl.BlockSpec(memory_space=pltpu.SMEM),
            pl.BlockSpec((1, block), lambda b: (0, b)),
            pl.BlockSpec((block, width), lambda b: (b, 0)),
        ],
        out_specs=[
            pl.BlockSpec((2, height, low), lambda b: (0, 0, 0)),
            pl.BlockSpec((height, low), lambda b: (0, 0)),
            pl.BlockSpec((height, low), lambda b: (0, 0)),
        ],
        out_shape=[
            jax.ShapeDtypeStruct((2, height, low), BF),
            jax.ShapeDtypeStruct((height, low), F32),
            jax.ShapeDtypeStruct((height, low), F32),
        ],
        scratch_shapes=[pltpu.VMEM((groups * width + PAD, low), F32)],
        compiler_params=pltpu.CompilerParams(vmem_limit_bytes=40 << 20),
        name="pool",
    )(scalars, ids, rows)


def attend_kernel(width, bits, digits, own_ref, got_ref, cand_ref, wq_ref, wk_ref, out_ref):
    queries = jnp.dot(cand_ref[...], wq_ref[...], preferred_element_type=F32).astype(BF)
    total = own_ref[...].astype(F32) + got_ref[...].astype(F32)
    centroids, keys, biases = [], [], []
    for k in range(2):
        count = jnp.zeros((1, total.shape[1]), F32)
        for d in range(digits):
            row = 2 * width + k * digits + d
            count = count + total[row : row + 1, :] * F32(2 ** (bits * d))
        here = (total[k * width : (k + 1) * width, :] / jnp.maximum(count, 1.0)).astype(BF)
        centroids.append(here)
        keys.append(
            lax.dot_general(wk_ref[...], here, TN, preferred_element_type=F32).astype(BF)
        )
        bias = jnp.where(count > 0, jnp.log(1.0 + count), F32(-1e9))
        biases.append(bias.astype(BF).astype(F32))
    centroids = jnp.concatenate(centroids, 1)
    keys = jnp.concatenate(keys, 1)
    biases = jnp.concatenate(biases, 1)
    scores = jnp.dot(queries, keys, preferred_element_type=F32) * F32(width**-0.5) + biases
    peak = jnp.max(scores, axis=1, keepdims=True)
    weights = jnp.exp(scores - peak)
    mass = jnp.sum(weights, axis=1, keepdims=True)
    attended = lax.dot_general(weights.astype(BF), centroids, NT, preferred_element_type=F32)
    level = peak + jnp.log(mass)
    first = level.astype(BF).astype(F32)
    second = (level - first).astype(BF).astype(F32)
    third = level - first - second
    lane = lax.broadcasted_iota(jnp.int32, attended.shape, 1)
    levels = jnp.where(lane == 0, first, jnp.where(lane == 1, second, jnp.where(lane == 2, third, 0.0)))
    out_ref[:, :width] = (attended / mass).astype(BF)
    out_ref[:, width:] = levels.astype(BF)


def attend(own, got, cands, w_query, w_key, bits, digits):
    width = w_key.shape[0]
    return pl.pallas_call(
        functools.partial(attend_kernel, width, bits, digits),
        out_shape=jax.ShapeDtypeStruct((cands.shape[0], 2 * width), BF),
        compiler_params=pltpu.CompilerParams(vmem_limit_bytes=24 << 20),
        name="attend",
    )(own, got, cands, w_query, w_key)


def rank_kernel(users, got_ref, cand_ref, wh_ref, bh_ref, wo_ref, out_ref):
    width = cand_ref.shape[2]
    local = cand_ref.shape[1]
    joined = []
    for user in range(users):
        parts, levels = [], []
        for r in range(SHARERS):
            one = got_ref[r * users + user].astype(F32)
            parts.append(one[:, :width])
            levels.append(jnp.sum(one[:, width:], axis=1, keepdims=True))
        peak = functools.reduce(jnp.maximum, levels)
        shares = [jnp.exp(level - peak) for level in levels]
        mass = functools.reduce(jnp.add, shares)
        top = functools.reduce(jnp.add, [s * p for s, p in zip(shares, parts)])
        joined.append((top / mass).astype(BF))
    attended = jnp.concatenate(joined, 0)
    cands = cand_ref[...].reshape(users * local, width)
    hidden = jnp.dot(cands, wh_ref[:width, :], preferred_element_type=F32)
    hidden = hidden + jnp.dot(attended, wh_ref[width:, :], preferred_element_type=F32)
    hidden = jnp.maximum(hidden + bh_ref[...], 0.0) * wo_ref[...]
    lanes = 128
    folded = functools.reduce(
        jnp.add, [hidden[:, k : k + lanes] for k in range(0, hidden.shape[1], lanes)]
    )
    ranking = jnp.sum(jnp.transpose(folded), axis=0, keepdims=True)
    for user in range(users):
        out_ref[user : user + 1, :] = ranking[:, user * local : (user + 1) * local]


def rank(got, cands, w_hidden, b_hidden, w_out):
    users, local, width = cands.shape
    return pl.pallas_call(
        functools.partial(rank_kernel, users),
        out_shape=jax.ShapeDtypeStruct((users, local), F32),
        compiler_params=pltpu.CompilerParams(vmem_limit_bytes=16 << 20),
        name="rank",
    )(got, cands, w_hidden, b_hidden.reshape(1, -1), w_out.reshape(1, -1))


def on_device(
    parts, users, behaviors, cluster_ids, lengths, candidates, w_query, w_key, w_hidden, b_hidden, w_out
):
    place = lax.axis_index("seq")
    flip = 4 * (place & 1) + (place & 2)
    scalars = jnp.stack([lengths[0, 0], flip.astype(jnp.int32)])
    bits, digits = digit_plan(parts, behaviors.shape[1])
    send, following, mine = pool(behaviors[0], cluster_ids, scalars, parts)

    def swap(value, step):
        return lax.ppermute(value, "seq", [(i, i ^ step) for i in range(parts)])

    pair = swap(send, 1).astype(F32)
    beside = swap((following + pair[1]).astype(BF), 2)
    total = mine + pair[0] + beside.astype(F32)
    own, step = total.astype(BF), SHARERS
    got = swap(own, step)
    candidates_in, got = lax.optimization_barrier((candidates, got))
    group = SHARERS * users
    groups = [[g * group + k for k in range(group)] for g in range(parts // SHARERS)]

    def exchange(value):
        return lax.all_to_all(
            value, ("seq", "cand"), 0, 0, tiled=True, axis_index_groups=groups
        )

    local, width = candidates.shape[1:]
    gathered = exchange(jnp.tile(candidates_in, (SHARERS, 1, 1)))
    while step * 2 < parts:
        step *= 2
        own = (own.astype(F32) + got.astype(F32)).astype(BF)
        got = swap(own, step)
    partial = attend(own, got, gathered.reshape(group * local, width), w_query, w_key, bits, digits)
    back = exchange(partial.reshape(group, local, 2 * width))
    return rank(back, candidates, w_hidden, b_hidden, w_out)


def solution(mesh):
    in_specs = (
        P("cand", "seq", None),
        P("cand", "seq"),
        P("cand", "seq"),
        P(None, ("seq", "cand"), None),
        P(),
        P(),
        P(),
        P(),
        P(),
    )
    out_specs = P(None, ("seq", "cand"))
    return jax.shard_map(
        functools.partial(on_device, mesh.shape["seq"], mesh.shape["cand"]),
        mesh=mesh,
        in_specs=in_specs,
        out_specs=out_specs,
        check_vma=False,
    )
```

time: 258 us -> 44.5 us (0.17)
  matrix products: 65.8 us -> 0 us
  waiting for transfers between devices: 53.8 us -> 8.54 us
  local copies, waits for them, and re-layouts: 38.8 us -> 2.98 us
  other arithmetic: 26.9 us -> 0.24 us
  blocking collectives: 41 us -> 15.6 us
  between operations: 13.5 us -> 0.75 us
  loops' own time: 12 us -> 0 us
  Pallas kernels: 0 us -> 7.96 us
  starting transfers between devices: 4.25 us -> 8.09 us
    dot_general x37 -> x0, matrix products: 65.8 us -> none  [the longest x16 39.4 us: accumulate(): lax.dot_general(onehot, lower, dims, preferred_element_type=jnp.float32)]
    psum x1 -> x0, waiting for transfers between devices: 53.7 us -> none  [on_device(): lax.psum(partials.astype(jnp.bfloat16), 'seq').astype(jnp.float32)]
    psum x1 -> x0, blocking collectives: 34.7 us -> none  [on_device(): lax.psum(counts.astype(jnp.bfloat16), 'seq').astype(jnp.float32)]
    convert_element_type x16 -> x0, local copies, waits for them, and re-layouts: 16.5 us -> none  [accumulate(): upper = lax.optimization_barrier(piece.astype(jnp.bfloat16))]
    reduce_sum x17 -> x0, other arithmetic: 14 us -> none  [the longest x16 13.7 us: accumulate(): tallies = tallies + jnp.sum(onehot, axis=0, dtype=jnp.float32)]
    another operation x1 -> x0, loops' own time: 12 us -> none  [cluster_partials(): lax.scan(accumulate, start, jnp.arange(slots // block_rows, dtype=jnp.int...]
    while x16 -> x0, local copies, waits for them, and re-layouts: 11 us -> none  [accumulate(): idents = lax.dynamic_slice_in_dim(cluster_ids, offset, block_rows, 0)]
    dynamic_slice x16 -> x0, local copies, waits for them, and re-layouts: 10.7 us -> none  [cluster_partials(): lax.scan(accumulate, start, jnp.arange(slots // block_rows, dtype=jnp.int...]
  transfers between devices with their start and end apart: 2 -> 4, of which waited for: 1 -> 3; matrix products, arithmetic and copies ran while one was open for 0% -> 0% of each run, Pallas kernels for 0% -> 0%
where the time goes in v1:
time: 44.5 us; the launch traced here: 44.2 us
  blocking collectives  15.6 us (35%)
  waiting for transfers between devices  8.54 us (19%)
  starting transfers between devices  8.09 us (18%)
  Pallas kernels  7.96 us (18%)
  local copies, waits for them, and re-layouts  2.98 us (7%)
  between operations  0.75 us (2%)
    all_to_all x2, blocking collectives, exchange(): lax.all_to_all(value, ('seq', 'cand'), 0, 0, tiled=True, axis_index_group...  15.6 us
    ppermute x4, waiting for transfers between devices, swap(): return lax.ppermute(value, 'seq', [(i, i ^ step) for i in range(parts)])  8.54 us
    ppermute x4, starting transfers between devices, swap(): return lax.ppermute(value, 'seq', [(i, i ^ step) for i in range(parts)])  8.09 us
    pallas_call x1, Pallas kernels, pool(): pl.pallas_call(functools.partial(pool_kernel, width, low, bits, digits),...  6.3 us
    unnamed x16, local copies, waits for them, and re-layouts  2.97 us
    pallas_call x1, Pallas kernels, rank(): pl.pallas_call(functools.partial(rank_kernel, users), out_shape=jax.Shape...  1.01 us
  transfers between devices with their start and end apart: 4, of which 3 were waited for; matrix products, arithmetic and copies ran while one was open for 0% of the time, Pallas kernels for 0%

profile of v1, /device:TPU:0, one launch (start us, length us, event | category | flops | bytes accessed | tf_op | source)
XLA Modules:
  0.0 44.2 jit_solution(13871107358214463546)
XLA Ops:
  0.0 0.0 copy-start.2
  0.0 0.0 copy-start.7
  0.0 0.0 copy-start.6
  0.7 0.1 pad_add_fusion.scalars
  0.8 0.0 copy-start
  0.8 2.2 %copy-done = f32[1,8192,128]{2,1,0:T(8,128)S(1)} copy-done((f32[1,8192,128]{2,1,0:T(8,128)S(1)}, f32[1,8192,128]{2,1,0:T(8,128)}, u32[]{:S(2)}) %copy-start) | copy-done | bytes 4194328
  3.0 0.0 copy-start.3
  3.0 0.8 %copy-done.3 = s32[1,8192]{1,0:T(1,128)S(1)} copy-done((s32[1,8192]{1,0:T(1,128)S(1)}, s32[1,8192]{1,0:T(1,128)}, u32[]{:S(2)}) %copy-start.3) | copy-done | bytes 32792
  3.7 0.0 copy-start.4
  3.7 0.0 copy-start.5
  3.7 0.0 copy-start.1
  3.7 6.3 %pool.1 = (bf16[2,272,256]{2,1,0:T(8,128)(2,1)S(1)}, f32[272,256]{1,0:T(8,128)S(1)}, f32[272,256]{1,0:T(8,128)S(1)}) custom-call(s32[2]{0:T(128)S(1)} %pad_add_fusion.scalars, s32[1,8192]{1,0:T(1,128)S(1)} %copy-done.3, f32[8192,128]{1,0:T(8,128)S(1)} %bitcast.23), custom_call_target="tpu_custom_call" | custom-call | tf_op jit(solution)/shard_map/pool/pallas_call | solution.py:90
  10.0 0.5 %collective-permute-start = (bf16[2,272,256]{2,1,0:T(8,128)(2,1)S(1)}, bf16[2,272,256]{2,1,0:T(8,128)(2,1)S(1)}, u32[]{:S(2)}, u32[]{:S(2)}) collective-permute-start(bf16[2,272,256]{2,1,0:T(8,128)(2,1)S(1)} %get-tuple-element.11), channel_id=1, source_target_pairs={{0,2},{2,0},{4,6},{6,4},{8,10},{10,8},{12,14},{14,12},{16,18},{18,... | collective-permute-start | bytes 835592 | tf_op jit(solution)/shard_map/ppermute | solution.py:207
  10.6 1.2 %collective-permute-done = bf16[2,272,256]{2,1,0:T(8,128)(2,1)S(1)} collective-permute-done((bf16[2,272,256]{2,1,0:T(8,128)(2,1)S(1)}, bf16[2,272,256]{2,1,0:T(8,128)(2,1)S(1)}, u32[]{:S(2)}, u32[]{:S(2)}) %collective-permute-start) | collective-permute-done | bytes 278560 | tf_op jit(solution)/shard_map/ppermute | solution.py:207
  11.8 2.9 %collective-permute-start.1 = (bf16[272,256]{1,0:T(8,128)(2,1)S(1)}, bf16[272,256]{1,0:T(8,128)(2,1)S(1)}, u32[]{:S(2)}, u32[]{:S(2)}) collective-permute-start(bf16[272,256]{1,0:T(8,128)(2,1)S(1)} %fusion.1), channel_id=1, source_target_pairs={{0,4},{2,6},{4,0},{6,2},{8,12},{10,14},{12,8},{14,10},{16,20},{18,... | collective-permute-start | bytes 417800 | tf_op jit(solution)/shard_map/ppermute | solution.py:207
  14.8 4.0 %collective-permute-done.1 = bf16[272,256]{1,0:T(8,128)(2,1)S(1)} collective-permute-done((bf16[272,256]{1,0:T(8,128)(2,1)S(1)}, bf16[272,256]{1,0:T(8,128)(2,1)S(1)}, u32[]{:S(2)}, u32[]{:S(2)}) %collective-permute-start.1) | collective-permute-done | bytes 139296 | tf_op jit(solution)/shard_map/ppermute | solution.py:207
  18.8 1.9 %collective-permute-start.2 = (bf16[272,256]{1,0:T(8,128)(2,1)S(1)}, bf16[272,256]{1,0:T(8,128)(2,1)S(1)}, u32[]{:S(2)}, u32[]{:S(2)}) collective-permute-start(bf16[272,256]{1,0:T(8,128)(2,1)S(1)} %fusion.4), channel_id=1, source_target_pairs={{0,8},{2,10},{4,12},{6,14},{8,0},{10,2},{12,4},{14,6},{16,24},{18,... | collective-permute-start | bytes 417800 | tf_op jit(solution)/shard_map/ppermute | solution.py:207
  20.7 3.4 %collective-permute-done.2 = bf16[272,256]{1,0:T(8,128)(2,1)S(1)} collective-permute-done((bf16[272,256]{1,0:T(8,128)(2,1)S(1)}, bf16[272,256]{1,0:T(8,128)(2,1)S(1)}, u32[]{:S(2)}, u32[]{:S(2)}) %collective-permute-start.2) | collective-permute-done | bytes 139296 | tf_op jit(solution)/shard_map/ppermute | solution.py:207
  24.1 2.8 %collective-permute-start.3 = (bf16[272,256]{1,0:T(8,128)(2,1)S(1)}, bf16[272,256]{1,0:T(8,128)(2,1)S(1)}, u32[]{:S(2)}, u32[]{:S(2)}) collective-permute-start(bf16[272,256]{1,0:T(8,128)(2,1)S(1)} %add_convert_fusion.own_ref), channel_id=1, source_target_pairs={{0,16},{2,18},{4,20},{6,22},{8,24},{10,26},{12,28},{14,30},{16,0},... | collective-permute-start | bytes 417800 | tf_op jit(solution)/shard_map/ppermute | solution.py:207
  26.8 0.0 copy-done.2
  26.9 8.3 %all_to_all.10 = bf16[8,32,128]{2,1,0:T(8,128)(2,1)S(1)} all-to-all(bf16[8,32,128]{2,1,0:T(8,128)(2,1)S(1)} %bitcast.28), channel_id=1, replica_groups={{0,1,2,3,4,5,6,7},{8,9,10,11,12,13,14,15},{16,17,18,19,20,21,22,23},{24..., dimensions={0} | all-to-all | bytes 131072 | tf_op jit(solution)/shard_map/all_to_all | solution.py:219
  35.1 0.0 collective-permute-done.3.got_ref
  35.1 0.0 copy-done.4
  35.1 0.0 copy-done.5
  35.1 0.6 %attend.1 = bf16[256,256]{1,0:T(8,128)(2,1)S(1)} custom-call(bf16[272,256]{1,0:T(8,128)(2,1)S(1)} %add_convert_fusion.own_ref, bf16[272,256]{1,0:T(8,128)(2,1)S(1)} %collective-permute-done.3.got_ref, bf16[256,128]{1,0:T(8,128)(2,1)S(1)} %bitcast.25, bf16[128,128]{1,0:T(8,128)(2,1)S(1)} %copy-done.4, bf16[128,128]{1,0:T(8,128)(2,1)S(1)} %copy-done.5), custom_call_target="tpu_custom_call" | custom-call | tf_op jit(solution)/shard_map/attend/pallas_call | solution.py:150
  35.8 7.3 %all_to_all.11.got_ref = bf16[8,32,256]{2,1,0:T(8,128)(2,1)S(1)} all-to-all(bf16[8,32,256]{2,1,0:T(8,128)(2,1)S(1)} %bitcast.24), channel_id=1, replica_groups={{0,1,2,3,4,5,6,7},{8,9,10,11,12,13,14,15},{16,17,18,19,20,21,22,23},{24..., dimensions={0} | all-to-all | bytes 262144 | tf_op jit(solution)/shard_map/all_to_all | solution.py:219
  43.1 0.0 copy-done.7
  43.1 0.0 copy-done.6
  43.1 0.0 copy-done.1
  43.1 1.0 %rank.1 = f32[2,32]{1,0:T(2,128)} custom-call(bf16[8,32,256]{2,1,0:T(8,128)(2,1)S(1)} %all_to_all.11.got_ref, bf16[2,32,128]{2,1,0:T(8,128)(2,1)S(1)} %copy-done.2, bf16[256,512]{1,0:T(8,128)(2,1)S(1)} %copy-done.1, f32[1,512]{1,0:T(1,128)S(1)} %bitcast.26, f32[1,512]{1,0:T(1,128)S(1)} %bitcast.27), custom_call_target="tpu_custom_call" | custom-call | tf_op jit(solution)/shard_map/rank/pallas_call | solution.py:189
  (5 shorter events, 0.2 us)
Async XLA Ops:
  0.0 26.8 %copy-start.2 = (bf16[2,32,128]{2,1,0:T(8,128)(2,1)S(1)}, bf16[2,32,128]{2,1,0:T(8,128)(2,1)}, u32[]{:S(2)}) copy-start(bf16[2,32,128]{2,1,0:T(8,128)(2,1)} %cand_ref.1) | copy-start | bytes 49156
  0.0 43.1 %copy-start.7 = (f32[512]{0:T(512)S(1)}, f32[512]{0:T(512)}, u32[]{:S(2)}) copy-start(f32[512]{0:T(512)} %param.17) | copy-start | bytes 6148
  0.0 43.1 %copy-start.6 = (f32[512]{0:T(512)S(1)}, f32[512]{0:T(512)}, u32[]{:S(2)}) copy-start(f32[512]{0:T(512)} %param.16) | copy-start | bytes 6148
  0.8 2.2 %copy-start = (f32[1,8192,128]{2,1,0:T(8,128)S(1)}, f32[1,8192,128]{2,1,0:T(8,128)}, u32[]{:S(2)}) copy-start(f32[1,8192,128]{2,1,0:T(8,128)} %param.9) | copy-start | bytes 12582916
  3.0 0.8 %copy-start.3 = (s32[1,8192]{1,0:T(1,128)S(1)}, s32[1,8192]{1,0:T(1,128)}, u32[]{:S(2)}) copy-start(s32[1,8192]{1,0:T(1,128)} %ids_ref.1) | copy-start | bytes 98308
  3.7 31.4 %copy-start.4 = (bf16[128,128]{1,0:T(8,128)(2,1)S(1)}, bf16[128,128]{1,0:T(8,128)(2,1)}, u32[]{:S(2)}) copy-start(bf16[128,128]{1,0:T(8,128)(2,1)} %wq_ref.1) | copy-start | bytes 98308
  3.7 31.4 %copy-start.5 = (bf16[128,128]{1,0:T(8,128)(2,1)S(1)}, bf16[128,128]{1,0:T(8,128)(2,1)}, u32[]{:S(2)}) copy-start(bf16[128,128]{1,0:T(8,128)(2,1)} %wk_ref.1) | copy-start | bytes 98308
  3.7 39.4 %copy-start.1 = (bf16[256,512]{1,0:T(8,128)(2,1)S(1)}, bf16[256,512]{1,0:T(8,128)(2,1)}, u32[]{:S(2)}) copy-start(bf16[256,512]{1,0:T(8,128)(2,1)} %wh_ref.1) | copy-start | bytes 786436
  10.0 1.7 %collective-permute-start = (bf16[2,272,256]{2,1,0:T(8,128)(2,1)S(1)}, bf16[2,272,256]{2,1,0:T(8,128)(2,1)S(1)}, u32[]{:S(2)}, u32[]{:S(2)}) collective-permute-start(bf16[2,272,256]{2,1,0:T(8,128)(2,1)S(1)} %get-tuple-element.11), channel_id=1, source_target_pairs={{0,2},{2,0},{4,6},{6,4},{8,10},{10,8},{12,14},{14,12},{16,18},{18,... | collective-permute-start | bytes 835592 | tf_op jit(solution)/shard_map/ppermute | solution.py:207
  11.8 6.9 %collective-permute-start.1 = (bf16[272,256]{1,0:T(8,128)(2,1)S(1)}, bf16[272,256]{1,0:T(8,128)(2,1)S(1)}, u32[]{:S(2)}, u32[]{:S(2)}) collective-permute-start(bf16[272,256]{1,0:T(8,128)(2,1)S(1)} %fusion.1), channel_id=1, source_target_pairs={{0,4},{2,6},{4,0},{6,2},{8,12},{10,14},{12,8},{14,10},{16,20},{18,... | collective-permute-start | bytes 417800 | tf_op jit(solution)/shard_map/ppermute | solution.py:207
  18.8 5.3 %collective-permute-start.2 = (bf16[272,256]{1,0:T(8,128)(2,1)S(1)}, bf16[272,256]{1,0:T(8,128)(2,1)S(1)}, u32[]{:S(2)}, u32[]{:S(2)}) collective-permute-start(bf16[272,256]{1,0:T(8,128)(2,1)S(1)} %fusion.4), channel_id=1, source_target_pairs={{0,8},{2,10},{4,12},{6,14},{8,0},{10,2},{12,4},{14,6},{16,24},{18,... | collective-permute-start | bytes 417800 | tf_op jit(solution)/shard_map/ppermute | solution.py:207
  24.1 11.0 %collective-permute-start.3 = (bf16[272,256]{1,0:T(8,128)(2,1)S(1)}, bf16[272,256]{1,0:T(8,128)(2,1)S(1)}, u32[]{:S(2)}, u32[]{:S(2)}) collective-permute-start(bf16[272,256]{1,0:T(8,128)(2,1)S(1)} %add_convert_fusion.own_ref), channel_id=1, source_target_pairs={{0,16},{2,18},{4,20},{6,22},{8,24},{10,26},{12,28},{14,30},{16,0},... | collective-permute-start | bytes 417800 | tf_op jit(solution)/shard_map/ppermute | solution.py:207

commit v2 on v1

v2 whole, which is shorter than its diff:
```python
import functools

import jax
import jax.numpy as jnp
from jax import lax
from jax.experimental import pallas as pl
from jax.experimental.pallas import tpu as pltpu
from jax.sharding import PartitionSpec as P

CLUSTERS = 2048
BF = jnp.bfloat16
F32 = jnp.float32
PAD = 16
SHARERS = 4
NT = (((1,), (1,)), ((), ()))
TN = (((0,), (0,)), ((), ()))
NN = (((1,), (0,)), ((), ()))


def digit_plan(parts, slots):
    bits = 1
    while parts * (2 ** (bits + 1) - 1) <= 256:
        bits += 1
    return bits, -(-(slots.bit_length()) // bits)


def split(ids, slots_before, live, flip, first, low):
    slot = slots_before + lax.broadcasted_iota(jnp.int32, ids.shape, 1)
    high = ((ids >> (low.bit_length() - 1)) ^ flip) - first
    high = jnp.where(slot < live, high, -PAD)
    return high.astype(F32).astype(BF), (ids & (low - 1)).astype(F32).astype(BF)


def labels(count):
    return lax.broadcasted_iota(jnp.int32, (count, 1), 0).astype(F32).astype(BF)


def pooled(turned, high, within, low, groups):
    onehot = jnp.where(labels(low) == within, BF(1), BF(0))
    pieces = [jnp.where(high == BF(h), turned, BF(0)) for h in range(groups)]
    pieces.append(jnp.where(labels(PAD) == high, BF(1), BF(0)))
    return lax.dot_general(jnp.concatenate(pieces, 0), onehot, NT, preferred_element_type=F32)


def give(total, width, bits, digits, dests):
    groups = 2 * len(dests)
    counts = total[groups * width :, :].astype(jnp.int32)
    row = lax.broadcasted_iota(jnp.int32, (PAD, 1), 0)
    for pair, dest in enumerate(dests):
        tally = jnp.zeros((PAD, total.shape[1]), jnp.int32)
        for k in range(2):
            for d in range(digits):
                one = (counts[2 * pair + k : 2 * pair + k + 1, :] >> (bits * d)) & (2**bits - 1)
                tally = jnp.where(row == k * digits + d, one, tally)
        dest[: 2 * width, :] = total[2 * pair * width : 2 * (pair + 1) * width, :].astype(dest.dtype)
        dest[2 * width :, :] = tally.astype(F32).astype(dest.dtype)


def flip_of(axis):
    place = lax.axis_index(axis)
    return (place & 1) * 2 + (place & 2) * 2


def far_kernel(low, bits, digits, live, ids_ref, rows_ref, send_ref, keep_ref, turned_ref, total):
    step, steps = pl.program_id(0), pl.num_programs(0)
    block, width = rows_ref.shape
    turned = jnp.transpose(rows_ref[...].astype(BF))
    turned_ref[...] = turned
    high, within = split(ids_ref[...], step * block, live[0, 0], flip_of("seq"), SHARERS, low)
    part = pooled(turned, high, within, low, SHARERS)

    @pl.when(step == 0)
    def _():
        total[...] = part

    @pl.when(step > 0)
    def _():
        total[...] += part

    @pl.when(step == steps - 1)
    def _():
        give(total[...], width, bits, digits, (keep_ref, send_ref))


def near_kernel(low, bits, digits, block, live, ids_ref, turned_ref, send_ref, keep_ref, total):
    width, slots = turned_ref.shape
    for start in range(0, slots, block):
        there = slice(start, start + block)
        high, within = split(ids_ref[:, there], start, live[0, 0], flip_of("seq"), 0, low)
        part = pooled(turned_ref[:, there], high, within, low, SHARERS)
        if start == 0:
            total[...] = part
        else:
            total[...] += part
    give(total[...], width, bits, digits, (keep_ref, send_ref))


def sizes(slots, width, parts):
    low = CLUSTERS // (2 * SHARERS)
    return low, SHARERS * width + PAD, 2 * width + PAD, digit_plan(parts, slots)


def pool_far(rows, ids, lengths, parts):
    slots, width = rows.shape
    low, tall, height, plan = sizes(slots, width, parts)
    block = min(4096, slots)
    return pl.pallas_call(
        functools.partial(far_kernel, low, *plan),
        grid=(slots // block,),
        in_specs=[
            pl.BlockSpec(memory_space=pltpu.SMEM),
            pl.BlockSpec((1, block), lambda b: (0, b)),
            pl.BlockSpec((block, width), lambda b: (b, 0)),
        ],
        out_specs=[
            pl.BlockSpec((height, low), lambda b: (0, 0)),
            pl.BlockSpec((height, low), lambda b: (0, 0)),
            pl.BlockSpec((width, block), lambda b: (0, b)),
        ],
        out_shape=[
            jax.ShapeDtypeStruct((height, low), BF),
            jax.ShapeDtypeStruct((height, low), F32),
            jax.ShapeDtypeStruct((width, slots), BF),
        ],
        scratch_shapes=[pltpu.VMEM((tall, low), F32)],
        compiler_params=pltpu.CompilerParams(vmem_limit_bytes=44 << 20),
        name="pool_far",
    )(
        lengths,
        pltpu.with_memory_space_constraint(ids, pltpu.HBM),
        pltpu.with_memory_space_constraint(rows, pltpu.HBM),
    )


def pool_near(turned, ids, lengths, parts):
    width, slots = turned.shape
    low, tall, height, plan = sizes(slots, width, parts)
    vmem = pl.BlockSpec(memory_space=pltpu.VMEM)
    return pl.pallas_call(
        functools.partial(near_kernel, low, *plan, min(2048, slots)),
        in_specs=[pl.BlockSpec(memory_space=pltpu.SMEM), vmem, vmem],
        out_specs=[vmem, vmem],
        out_shape=[
            jax.ShapeDtypeStruct((height, low), BF),
            jax.ShapeDtypeStruct((height, low), F32),
        ],
        scratch_shapes=[pltpu.VMEM((tall, low), F32)],
        compiler_params=pltpu.CompilerParams(vmem_limit_bytes=44 << 20),
        name="pool_near",
    )(lengths, ids, turned)


def attend_kernel(width, users, bits, digits, own_ref, got_ref, cand_ref, other_ref, wq_ref, wk_ref, out_ref):
    cands = jnp.concatenate([cand_ref[...], other_ref[...]], 0)
    queries = jnp.dot(cands, wq_ref[...], preferred_element_type=F32).astype(BF)
    total = own_ref[...].astype(F32) + got_ref[...].astype(F32)
    centroids, keys, biases = [], [], []
    for k in range(2):
        count = jnp.zeros((1, total.shape[1]), F32)
        for d in range(digits):
            row = 2 * width + k * digits + d
            count = count + total[row : row + 1, :] * F32(2 ** (bits * d))
        here = (total[k * width : (k + 1) * width, :] / jnp.maximum(count, 1.0)).astype(BF)
        centroids.append(here)
        keys.append(
            lax.dot_general(wk_ref[...], here, TN, preferred_element_type=F32).astype(BF)
        )
        bias = jnp.where(count > 0, jnp.log(1.0 + count), F32(-1e9))
        biases.append(bias.astype(BF).astype(F32))
    centroids = jnp.concatenate(centroids, 1)
    keys = jnp.concatenate(keys, 1)
    biases = jnp.concatenate(biases, 1)
    scores = jnp.dot(queries, keys, preferred_element_type=F32) * F32(width**-0.5) + biases
    peak = jnp.max(scores, axis=1, keepdims=True)
    weights = jnp.exp(scores - peak)
    mass = jnp.sum(weights, axis=1, keepdims=True)
    attended = lax.dot_general(weights.astype(BF), centroids, NT, preferred_element_type=F32)
    level = peak + jnp.log(mass)
    first = level.astype(BF).astype(F32)
    second = (level - first).astype(BF).astype(F32)
    third = level - first - second
    lane = lax.broadcasted_iota(jnp.int32, attended.shape, 1)
    levels = jnp.where(lane == 0, first, jnp.where(lane == 1, second, jnp.where(lane == 2, third, 0.0)))
    result = jnp.concatenate([(attended / mass).astype(BF), levels.astype(BF)], 1)
    local = out_ref.shape[1]
    place, user = lax.axis_index("seq") & (SHARERS - 1), lax.axis_index("cand")
    for r in range(SHARERS):
        for u in range(users):
            start = (r * users + u) * local
            out_ref[(place ^ r) * users + (user ^ u)] = result[start : start + local, :]


def attend(own, got, cands, others, w_query, w_key, users, bits, digits):
    width = w_key.shape[0]
    group = SHARERS * users
    return pl.pallas_call(
        functools.partial(attend_kernel, width, users, bits, digits),
        out_shape=jax.ShapeDtypeStruct((group, 2 * cands.shape[0] // group, 2 * width), BF),
        compiler_params=pltpu.CompilerParams(vmem_limit_bytes=24 << 20),
        name="attend",
    )(own, got, cands, others, w_query, w_key)


def rank_kernel(users, got_ref, cand_ref, wh_ref, bh_ref, wo_ref, out_ref):
    width = cand_ref.shape[2]
    local = cand_ref.shape[1]
    joined = []
    for user in range(users):
        parts, levels = [], []
        for r in range(SHARERS):
            one = got_ref[r * users + user].astype(F32)
            parts.append(one[:, :width])
            levels.append(jnp.sum(one[:, width:], axis=1, keepdims=True))
        peak = functools.reduce(jnp.maximum, levels)
        shares = [jnp.exp(level - peak) for level in levels]
        mass = functools.reduce(jnp.add, shares)
        top = functools.reduce(jnp.add, [s * p for s, p in zip(shares, parts)])
        joined.append((top / mass).astype(BF))
    attended = jnp.concatenate(joined, 0)
    cands = cand_ref[...].reshape(users * local, width)
    hidden = jnp.dot(cands, wh_ref[:width, :], preferred_element_type=F32)
    hidden = hidden + jnp.dot(attended, wh_ref[width:, :], preferred_element_type=F32)
    hidden = jnp.maximum(hidden + bh_ref[...], 0.0) * wo_ref[...]
    lanes = 128
    folded = functools.reduce(
        jnp.add, [hidden[:, k : k + lanes] for k in range(0, hidden.shape[1], lanes)]
    )
    ranking = jnp.sum(jnp.transpose(folded), axis=0, keepdims=True)
    for user in range(users):
        out_ref[user : user + 1, :] = ranking[:, user * local : (user + 1) * local]


def rank(got, cands, w_hidden, b_hidden, w_out):
    users, local, width = cands.shape
    return pl.pallas_call(
        functools.partial(rank_kernel, users),
        out_shape=jax.ShapeDtypeStruct((users, local), F32),
        compiler_params=pltpu.CompilerParams(vmem_limit_bytes=16 << 20),
        name="rank",
    )(got, cands, w_hidden, b_hidden.reshape(1, -1), w_out.reshape(1, -1))


def on_device(
    parts, users, behaviors, cluster_ids, lengths, candidates, w_query, w_key, w_hidden, b_hidden, w_out
):
    bits, digits = digit_plan(parts, behaviors.shape[1])

    def swap(value, step, axis="seq", count=parts):
        return lax.ppermute(value, axis, [(i, i ^ step) for i in range(count)])

    def after(value, earlier):
        return lax.optimization_barrier((value, earlier))

    send, beyond, turned = pool_far(behaviors[0], cluster_ids, lengths, parts)
    got = swap(send, 1)
    turned, got = after(turned, got)
    beside = swap((beyond + got.astype(F32)).astype(BF), 2)
    send, mine = pool_near(turned, cluster_ids, lengths, parts)
    candidates_in, send = after(candidates, send)
    got = swap(send, 1)
    asked = jnp.stack([candidates_in, swap(candidates_in, 1)], 1)
    own = (mine + got.astype(F32) + beside.astype(F32)).astype(BF)
    asked, own = after(asked, own)
    step = SHARERS
    got = swap(own, step)
    user = lax.axis_index("cand")
    asked = [lax.dynamic_index_in_dim(asked, user ^ u, 0, False) for u in range(users)]
    asked = asked[:1] + [swap(asked[u], u, "cand", users) for u in range(1, users)]
    asked = jnp.stack(asked, 1).reshape(2 * users * candidates.shape[1], -1)
    while step * 2 < parts:
        step *= 2
        own = (own.astype(F32) + got.astype(F32)).astype(BF)
        asked, own = after(asked, own)
        got = swap(own, step)
    partial = attend(own, got, asked, swap(asked, 2), w_query, w_key, users, bits, digits)
    group = SHARERS * users
    groups = [[g * group + k for k in range(group)] for g in range(parts // SHARERS)]
    back = lax.all_to_all(partial, ("seq", "cand"), 0, 0, tiled=True, axis_index_groups=groups)
    return rank(back, candidates, w_hidden, b_hidden, w_out)


def solution(mesh):
    in_specs = (
        P("cand", "seq", None),
        P("cand", "seq"),
        P("cand", "seq"),
        P(None, ("seq", "cand"), None),
        P(),
        P(),
        P(),
        P(),
        P(),
    )
    out_specs = P(None, ("seq", "cand"))
    return jax.shard_map(
        functools.partial(on_device, mesh.shape["seq"], mesh.shape["cand"]),
        mesh=mesh,
        in_specs=in_specs,
        out_specs=out_specs,
        check_vma=False,
    )
```

time: 44.5 us -> 38 us (0.85)
  blocking collectives: 15.6 us -> 7.34 us
  starting transfers between devices: 8.09 us -> 11.3 us
  local copies, waits for them, and re-layouts: 2.98 us -> 0.03 us
  waiting for transfers between devices: 8.54 us -> 9.51 us
  Pallas kernels: 7.96 us -> 8.75 us
    all_to_all x2 -> x1, blocking collectives: 15.6 us -> 7.34 us  [on_device(): lax.all_to_all(partial, ('seq', 'cand'), 0, 0, tiled=True, axis_index_gro...]
    ppermute x4 -> x8, starting transfers between devices: 8.09 us -> 11.3 us  [swap(): return lax.ppermute(value, axis, [(i, i ^ step) for i in range(count)])]
    unnamed x16 -> x14, local copies, waits for them, and re-layouts: 2.97 us -> 0.03 us
    ppermute x4 -> x8, waiting for transfers between devices: 8.54 us -> 9.51 us  [swap(): return lax.ppermute(value, axis, [(i, i ^ step) for i in range(count)])]
    pallas_call x2 -> x3, Pallas kernels: 6.95 us -> 7.74 us  [the longest x1 4.64 us: pool_far(): pl.pallas_call(functools.partial(far_kernel, low, *plan), grid=(slots //...]
  transfers between devices with their start and end apart: 4 -> 8, of which waited for: 3 -> 7; matrix products, arithmetic and copies ran while one was open for 0% -> 0% of each run, Pallas kernels for 0% -> 6%
where the time goes in v2:
time: 38 us; the launch traced here: 37.8 us
  starting transfers between devices  11.3 us (30%)
  waiting for transfers between devices  9.51 us (25%)
  Pallas kernels  8.75 us (23%)
  blocking collectives  7.34 us (19%)
  between operations  0.76 us (2%)
    ppermute x8, starting transfers between devices, swap(): return lax.ppermute(value, axis, [(i, i ^ step) for i in range(count)])  11.3 us
    ppermute x8, waiting for transfers between devices, swap(): return lax.ppermute(value, axis, [(i, i ^ step) for i in range(count)])  9.51 us
    all_to_all x1, blocking collectives, on_device(): lax.all_to_all(partial, ('seq', 'cand'), 0, 0, tiled=True, axis_index_gro...  7.34 us
    pallas_call x1, Pallas kernels, pool_far(): pl.pallas_call(functools.partial(far_kernel, low, *plan), grid=(slots //...  4.64 us
    pallas_call x1, Pallas kernels, pool_near(): pl.pallas_call(functools.partial(near_kernel, low, *plan, min(2048, slots...  2.45 us
    pallas_call x1, Pallas kernels, rank(): pl.pallas_call(functools.partial(rank_kernel, users), out_shape=jax.Shape...  1.01 us
  transfers between devices with their start and end apart: 8, of which 7 were waited for; matrix products, arithmetic and copies ran while one was open for 0% of the time, Pallas kernels for 6%

profile of v2, /device:TPU:0, one launch (start us, length us, event | category | flops | bytes accessed | tf_op | source)
XLA Modules:
  0.0 37.8 jit_solution(10710447986622659495)
XLA Ops:
  0.0 0.0 copy-start.1
  0.7 0.0 copy-start
  0.7 0.0 copy-start.5
  0.7 0.0 copy-start.6
  0.7 4.6 %pool_far.1 = (bf16[272,256]{1,0:T(8,128)(2,1)S(1)}, f32[272,256]{1,0:T(8,128)S(1)}, bf16[128,8192]{1,0:T(8,128)(2,1)S(1)}) custom-call(s32[1,1]{1,0:T(1,128)S(6)} %copy.10.live, s32[1,8192]{1,0:T(1,128)} %ids_ref.3, f32[8192,128]{1,0:T(8,128)} %bitcast.16), custom_call_target="tpu_custom_call" | custom-call | tf_op jit(solution)/shard_map/pool_far/pallas_call | solution.py:107
  5.4 0.5 %collective-permute-start = (bf16[272,256]{1,0:T(8,128)(2,1)S(1)}, bf16[272,256]{1,0:T(8,128)(2,1)S(1)}, u32[]{:S(2)}, u32[]{:S(2)}) collective-permute-start(bf16[272,256]{1,0:T(8,128)(2,1)S(1)} %get-tuple-element.19), channel_id=1, source_target_pairs={{0,2},{2,0},{4,6},{6,4},{8,10},{10,8},{12,14},{14,12},{16,18},{18,... | collective-permute-start | bytes 417800 | tf_op jit(solution)/shard_map/ppermute | solution.py:249
  5.9 1.0 %collective-permute-done = bf16[272,256]{1,0:T(8,128)(2,1)S(1)} collective-permute-done((bf16[272,256]{1,0:T(8,128)(2,1)S(1)}, bf16[272,256]{1,0:T(8,128)(2,1)S(1)}, u32[]{:S(2)}, u32[]{:S(2)}) %collective-permute-start) | collective-permute-done | bytes 139296 | tf_op jit(solution)/shard_map/ppermute | solution.py:249
  6.9 2.9 %collective-permute-start.3 = (bf16[272,256]{1,0:T(8,128)(2,1)S(1)}, bf16[272,256]{1,0:T(8,128)(2,1)S(1)}, u32[]{:S(2)}, u32[]{:S(2)}) collective-permute-start(bf16[272,256]{1,0:T(8,128)(2,1)S(1)} %add_convert_fusion.2), channel_id=1, source_target_pairs={{0,4},{2,6},{4,0},{6,2},{8,12},{10,14},{12,8},{14,10},{16,20},{18,... | collective-permute-start | bytes 417800 | tf_op jit(solution)/shard_map/ppermute | solution.py:249
  9.8 0.0 copy-done.1
  9.8 2.5 %pool_near.1 = (bf16[272,256]{1,0:T(8,128)(2,1)S(1)}, f32[272,256]{1,0:T(8,128)S(1)}) custom-call(s32[1,1]{1,0:T(1,128)S(6)} %copy.10.live, s32[1,8192]{1,0:T(1,128)S(1)} %copy-done.1, bf16[128,8192]{1,0:T(8,128)(2,1)S(1)} %get-tuple-element.20.turned_ref), custom_call_target="tpu_custom_call" | custom-call | tf_op jit(solution)/shard_map/pool_near/pallas_call | solution.py:139
  12.3 0.1 collective-permute-start.2
  12.4 0.0 copy-done.2
  12.4 0.5 %collective-permute-start.1 = (bf16[2,32,128]{2,1,0:T(8,128)(2,1)S(1)}, bf16[2,32,128]{2,1,0:T(8,128)(2,1)S(1)}, u32[]{:S(2)}, u32[]{:S(2)}) collective-permute-start(bf16[2,32,128]{2,1,0:T(8,128)(2,1)S(1)} %copy-done.2), channel_id=1, source_target_pairs={{0,2},{2,0},{4,6},{6,4},{8,10},{10,8},{12,14},{14,12},{16,18},{18,... | collective-permute-start | bytes 49160 | tf_op jit(solution)/shard_map/ppermute | solution.py:249
  12.9 0.9 %collective-permute-done.1 = bf16[2,32,128]{2,1,0:T(8,128)(2,1)S(1)} collective-permute-done((bf16[2,32,128]{2,1,0:T(8,128)(2,1)S(1)}, bf16[2,32,128]{2,1,0:T(8,128)(2,1)S(1)}, u32[]{:S(2)}, u32[]{:S(2)}) %collective-permute-start.1) | collective-permute-done | bytes 16416 | tf_op jit(solution)/shard_map/ppermute | solution.py:249
  13.7 0.1 collective-permute-done.3
  13.8 0.0 collective-permute-done.2
  13.9 1.9 %collective-permute-start.5 = (bf16[272,256]{1,0:T(8,128)(2,1)S(1)}, bf16[272,256]{1,0:T(8,128)(2,1)S(1)}, u32[]{:S(2)}, u32[]{:S(2)}) collective-permute-start(bf16[272,256]{1,0:T(8,128)(2,1)S(1)} %add_convert_fusion.1), channel_id=1, source_target_pairs={{0,8},{2,10},{4,12},{6,14},{8,0},{10,2},{12,4},{14,6},{16,24},{18,... | collective-permute-start | bytes 417800 | tf_op jit(solution)/shard_map/ppermute | solution.py:249
  15.8 1.5 %collective-permute-start.4 = (bf16[2,32,128]{2,1,0:T(8,128)(2,1)S(1)}, bf16[2,32,128]{2,1,0:T(8,128)(2,1)S(1)}, u32[]{:S(2)}, u32[]{:S(2)}) collective-permute-start(bf16[2,32,128]{2,1,0:T(8,128)(2,1)S(1)} %get-tuple-element.32), channel_id=1, source_target_pairs={{0,1},{1,0},{2,3},{3,2},{4,5},{5,4},{6,7},{7,6},{8,9},{9,8},{10,11... | collective-permute-start | bytes 49160 | tf_op jit(solution)/shard_map/ppermute | solution.py:249
  17.3 2.2 %collective-permute-done.4 = bf16[2,32,128]{2,1,0:T(8,128)(2,1)S(1)} collective-permute-done((bf16[2,32,128]{2,1,0:T(8,128)(2,1)S(1)}, bf16[2,32,128]{2,1,0:T(8,128)(2,1)S(1)}, u32[]{:S(2)}, u32[]{:S(2)}) %collective-permute-start.4) | collective-permute-done | bytes 16416 | tf_op jit(solution)/shard_map/ppermute | solution.py:249
  19.5 0.3 collective-permute-done.5
  19.8 2.7 %collective-permute-start.6 = (bf16[272,256]{1,0:T(8,128)(2,1)S(1)}, bf16[272,256]{1,0:T(8,128)(2,1)S(1)}, u32[]{:S(2)}, u32[]{:S(2)}) collective-permute-start(bf16[272,256]{1,0:T(8,128)(2,1)S(1)} %add_convert_fusion.own_ref), channel_id=1, source_target_pairs={{0,16},{2,18},{4,20},{6,22},{8,24},{10,26},{12,28},{14,30},{16,0},... | collective-permute-start | bytes 417800 | tf_op jit(solution)/shard_map/ppermute | solution.py:249
  22.5 1.2 %collective-permute-start.7 = (bf16[128,128]{1,0:T(8,128)(2,1)S(1)}, bf16[128,128]{1,0:T(8,128)(2,1)S(1)}, u32[]{:S(2)}, u32[]{:S(2)}) collective-permute-start(bf16[128,128]{1,0:T(8,128)(2,1)S(1)} %bitcast.11), channel_id=1, source_target_pairs={{0,4},{2,6},{4,0},{6,2},{8,12},{10,14},{12,8},{14,10},{16,20},{18,... | collective-permute-start | bytes 98312 | tf_op jit(solution)/shard_map/ppermute | solution.py:249
  23.7 2.7 %collective-permute-done.7.other_ref = bf16[128,128]{1,0:T(8,128)(2,1)S(1)} collective-permute-done((bf16[128,128]{1,0:T(8,128)(2,1)S(1)}, bf16[128,128]{1,0:T(8,128)(2,1)S(1)}, u32[]{:S(2)}, u32[]{:S(2)}) %collective-permute-start.7) | collective-permute-done | bytes 32800 | tf_op jit(solution)/shard_map/ppermute | solution.py:249
  26.4 2.4 %collective-permute-done.6.got_ref = bf16[272,256]{1,0:T(8,128)(2,1)S(1)} collective-permute-done((bf16[272,256]{1,0:T(8,128)(2,1)S(1)}, bf16[272,256]{1,0:T(8,128)(2,1)S(1)}, u32[]{:S(2)}, u32[]{:S(2)}) %collective-permute-start.6) | collective-permute-done | bytes 139296 | tf_op jit(solution)/shard_map/ppermute | solution.py:249
  28.8 0.0 copy-done.3
  28.8 0.0 copy-done.4
  28.8 0.6 %attend.1 = bf16[8,32,256]{2,1,0:T(8,128)(2,1)S(1)} custom-call(bf16[272,256]{1,0:T(8,128)(2,1)S(1)} %add_convert_fusion.own_ref, bf16[272,256]{1,0:T(8,128)(2,1)S(1)} %collective-permute-done.6.got_ref, bf16[128,128]{1,0:T(8,128)(2,1)S(1)} %bitcast.12, bf16[128,128]{1,0:T(8,128)(2,1)S(1)} %collective-permute-done.7.other_ref, ...), custom_call_target="tpu_custom_call" | custom-call | tf_op jit(solution)/shard_map/attend/pallas_call | solution.py:196
  29.4 7.3 %all_to_all.5.got_ref = bf16[8,32,256]{2,1,0:T(8,128)(2,1)S(1)} all-to-all(bf16[8,32,256]{2,1,0:T(8,128)(2,1)S(1)} %attend.1), channel_id=1, replica_groups={{0,1,2,3,4,5,6,7},{8,9,10,11,12,13,14,15},{16,17,18,19,20,21,22,23},{24..., dimensions={0} | all-to-all | bytes 262144 | tf_op jit(solution)/shard_map/all_to_all | solution.py:278
  36.8 0.0 copy-done
  36.8 0.0 copy-done.5
  36.8 0.0 copy-done.6
  36.8 1.0 %rank.1 = f32[2,32]{1,0:T(2,128)} custom-call(bf16[8,32,256]{2,1,0:T(8,128)(2,1)S(1)} %all_to_all.5.got_ref, bf16[2,32,128]{2,1,0:T(8,128)(2,1)S(1)} %copy-done.2, bf16[256,512]{1,0:T(8,128)(2,1)S(1)} %copy-done, f32[1,512]{1,0:T(1,128)S(1)} %bitcast.14, f32[1,512]{1,0:T(1,128)S(1)} %bitcast.15), custom_call_target="tpu_custom_call" | custom-call | tf_op jit(solution)/shard_map/rank/pallas_call | solution.py:235
  (9 shorter events, 0.1 us)
Async XLA Ops:
  0.0 9.8 %copy-start.1 = (s32[1,8192]{1,0:T(1,128)S(1)}, s32[1,8192]{1,0:T(1,128)}, u32[]{:S(2)}) copy-start(s32[1,8192]{1,0:T(1,128)} %ids_ref.3) | copy-start | bytes 98308
  0.0 12.4 %copy-start.2 = (bf16[2,32,128]{2,1,0:T(8,128)(2,1)S(1)}, bf16[2,32,128]{2,1,0:T(8,128)(2,1)}, u32[]{:S(2)}) copy-start(bf16[2,32,128]{2,1,0:T(8,128)(2,1)} %cand_ref.1) | copy-start | bytes 49156
  0.0 28.8 %copy-start.3 = (bf16[128,128]{1,0:T(8,128)(2,1)S(1)}, bf16[128,128]{1,0:T(8,128)(2,1)}, u32[]{:S(2)}) copy-start(bf16[128,128]{1,0:T(8,128)(2,1)} %wq_ref.1) | copy-start | bytes 98308
  0.0 28.8 %copy-start.4 = (bf16[128,128]{1,0:T(8,128)(2,1)S(1)}, bf16[128,128]{1,0:T(8,128)(2,1)}, u32[]{:S(2)}) copy-start(bf16[128,128]{1,0:T(8,128)(2,1)} %wk_ref.1) | copy-start | bytes 98308
  0.7 36.1 %copy-start = (bf16[256,512]{1,0:T(8,128)(2,1)S(1)}, bf16[256,512]{1,0:T(8,128)(2,1)}, u32[]{:S(2)}) copy-start(bf16[256,512]{1,0:T(8,128)(2,1)} %wh_ref.1) | copy-start | bytes 786436
  0.7 36.1 %copy-start.5 = (f32[512]{0:T(512)S(1)}, f32[512]{0:T(512)}, u32[]{:S(2)}) copy-start(f32[512]{0:T(512)} %param.16) | copy-start | bytes 6148
  0.7 36.1 %copy-start.6 = (f32[512]{0:T(512)S(1)}, f32[512]{0:T(512)}, u32[]{:S(2)}) copy-start(f32[512]{0:T(512)} %param.17) | copy-start | bytes 6148
  5.4 1.5 %collective-permute-start = (bf16[272,256]{1,0:T(8,128)(2,1)S(1)}, bf16[272,256]{1,0:T(8,128)(2,1)S(1)}, u32[]{:S(2)}, u32[]{:S(2)}) collective-permute-start(bf16[272,256]{1,0:T(8,128)(2,1)S(1)} %get-tuple-element.19), channel_id=1, source_target_pairs={{0,2},{2,0},{4,6},{6,4},{8,10},{10,8},{12,14},{14,12},{16,18},{18,... | collective-permute-start | bytes 417800 | tf_op jit(solution)/shard_map/ppermute | solution.py:249
  6.9 6.9 %collective-permute-start.3 = (bf16[272,256]{1,0:T(8,128)(2,1)S(1)}, bf16[272,256]{1,0:T(8,128)(2,1)S(1)}, u32[]{:S(2)}, u32[]{:S(2)}) collective-permute-start(bf16[272,256]{1,0:T(8,128)(2,1)S(1)} %add_convert_fusion.2), channel_id=1, source_target_pairs={{0,4},{2,6},{4,0},{6,2},{8,12},{10,14},{12,8},{14,10},{16,20},{18,... | collective-permute-start | bytes 417800 | tf_op jit(solution)/shard_map/ppermute | solution.py:249
  12.3 1.5 %collective-permute-start.2 = (bf16[272,256]{1,0:T(8,128)(2,1)S(1)}, bf16[272,256]{1,0:T(8,128)(2,1)S(1)}, u32[]{:S(2)}, u32[]{:S(2)}) collective-permute-start(bf16[272,256]{1,0:T(8,128)(2,1)S(1)} %get-tuple-element.24), channel_id=1, source_target_pairs={{0,2},{2,0},{4,6},{6,4},{8,10},{10,8},{12,14},{14,12},{16,18},{18,... | collective-permute-start | bytes 417800 | tf_op jit(solution)/shard_map/ppermute | solution.py:249
  12.4 1.4 %collective-permute-start.1 = (bf16[2,32,128]{2,1,0:T(8,128)(2,1)S(1)}, bf16[2,32,128]{2,1,0:T(8,128)(2,1)S(1)}, u32[]{:S(2)}, u32[]{:S(2)}) collective-permute-start(bf16[2,32,128]{2,1,0:T(8,128)(2,1)S(1)} %copy-done.2), channel_id=1, source_target_pairs={{0,2},{2,0},{4,6},{6,4},{8,10},{10,8},{12,14},{14,12},{16,18},{18,... | collective-permute-start | bytes 49160 | tf_op jit(solution)/shard_map/ppermute | solution.py:249
  13.9 5.9 %collective-permute-start.5 = (bf16[272,256]{1,0:T(8,128)(2,1)S(1)}, bf16[272,256]{1,0:T(8,128)(2,1)S(1)}, u32[]{:S(2)}, u32[]{:S(2)}) collective-permute-start(bf16[272,256]{1,0:T(8,128)(2,1)S(1)} %add_convert_fusion.1), channel_id=1, source_target_pairs={{0,8},{2,10},{4,12},{6,14},{8,0},{10,2},{12,4},{14,6},{16,24},{18,... | collective-permute-start | bytes 417800 | tf_op jit(solution)/shard_map/ppermute | solution.py:249
  15.8 3.7 %collective-permute-start.4 = (bf16[2,32,128]{2,1,0:T(8,128)(2,1)S(1)}, bf16[2,32,128]{2,1,0:T(8,128)(2,1)S(1)}, u32[]{:S(2)}, u32[]{:S(2)}) collective-permute-start(bf16[2,32,128]{2,1,0:T(8,128)(2,1)S(1)} %get-tuple-element.32), channel_id=1, source_target_pairs={{0,1},{1,0},{2,3},{3,2},{4,5},{5,4},{6,7},{7,6},{8,9},{9,8},{10,11... | collective-permute-start | bytes 49160 | tf_op jit(solution)/shard_map/ppermute | solution.py:249
  19.8 9.0 %collective-permute-start.6 = (bf16[272,256]{1,0:T(8,128)(2,1)S(1)}, bf16[272,256]{1,0:T(8,128)(2,1)S(1)}, u32[]{:S(2)}, u32[]{:S(2)}) collective-permute-start(bf16[272,256]{1,0:T(8,128)(2,1)S(1)} %add_convert_fusion.own_ref), channel_id=1, source_target_pairs={{0,16},{2,18},{4,20},{6,22},{8,24},{10,26},{12,28},{14,30},{16,0},... | collective-permute-start | bytes 417800 | tf_op jit(solution)/shard_map/ppermute | solution.py:249
  22.5 3.9 %collective-permute-start.7 = (bf16[128,128]{1,0:T(8,128)(2,1)S(1)}, bf16[128,128]{1,0:T(8,128)(2,1)S(1)}, u32[]{:S(2)}, u32[]{:S(2)}) collective-permute-start(bf16[128,128]{1,0:T(8,128)(2,1)S(1)} %bitcast.11), channel_id=1, source_target_pairs={{0,4},{2,6},{4,0},{6,2},{8,12},{10,14},{12,8},{14,10},{16,20},{18,... | collective-permute-start | bytes 98312 | tf_op jit(solution)/shard_map/ppermute | solution.py:249

commit v3 on v2

--- a/solution.py
+++ b/solution.py
@@ -146,6 +146,9 @@
         ],
         scratch_shapes=[pltpu.VMEM((tall, low), F32)],
         compiler_params=pltpu.CompilerParams(vmem_limit_bytes=44 << 20),
+        cost_estimate=pl.CostEstimate(
+            flops=2 * tall * low * slots, bytes_accessed=2 * width * slots, transcendentals=0
+        ),
         name="pool_near",
     )(lengths, ids, turned)
 
@@ -201,9 +204,9 @@
     )(own, got, cands, others, w_query, w_key)
 
 
-def rank_kernel(users, got_ref, cand_ref, wh_ref, bh_ref, wo_ref, out_ref):
-    width = cand_ref.shape[2]
-    local = cand_ref.shape[1]
+def rank_kernel(users, got_ref, base_ref, wh_ref, wo_ref, out_ref):
+    width = got_ref.shape[2] // 2
+    local = got_ref.shape[1]
     joined = []
     for user in range(users):
         parts, levels = [], []
@@ -217,10 +220,8 @@
         top = functools.reduce(jnp.add, [s * p for s, p in zip(shares, parts)])
         joined.append((top / mass).astype(BF))
     attended = jnp.concatenate(joined, 0)
-    cands = cand_ref[...].reshape(users * local, width)
-    hidden = jnp.dot(cands, wh_ref[:width, :], preferred_element_type=F32)
-    hidden = hidden + jnp.dot(attended, wh_ref[width:, :], preferred_element_type=F32)
-    hidden = jnp.maximum(hidden + bh_ref[...], 0.0) * wo_ref[...]
+    hidden = base_ref[...] + jnp.dot(attended, wh_ref[width:, :], preferred_element_type=F32)
+    hidden = jnp.maximum(hidden, 0.0) * wo_ref[...]
     lanes = 128
     folded = functools.reduce(
         jnp.add, [hidden[:, k : k + lanes] for k in range(0, hidden.shape[1], lanes)]
@@ -230,14 +231,13 @@
         out_ref[user : user + 1, :] = ranking[:, user * local : (user + 1) * local]
 
 
-def rank(got, cands, w_hidden, b_hidden, w_out):
-    users, local, width = cands.shape
+def rank(got, base, w_hidden, w_out, users):
     return pl.pallas_call(
         functools.partial(rank_kernel, users),
-        out_shape=jax.ShapeDtypeStruct((users, local), F32),
+        out_shape=jax.ShapeDtypeStruct((users, got.shape[1]), F32),
         compiler_params=pltpu.CompilerParams(vmem_limit_bytes=16 << 20),
         name="rank",
-    )(got, cands, w_hidden, b_hidden.reshape(1, -1), w_out.reshape(1, -1))
+    )(got, base, w_hidden, w_out.reshape(1, -1))
 
 
 def on_device(
@@ -251,32 +251,36 @@
     def after(value, earlier):
         return lax.optimization_barrier((value, earlier))
 
+    user = lax.axis_index("cand")
     send, beyond, turned = pool_far(behaviors[0], cluster_ids, lengths, parts)
     got = swap(send, 1)
     turned, got = after(turned, got)
     beside = swap((beyond + got.astype(F32)).astype(BF), 2)
     send, mine = pool_near(turned, cluster_ids, lengths, parts)
-    candidates_in, send = after(candidates, send)
     got = swap(send, 1)
-    asked = jnp.stack([candidates_in, swap(candidates_in, 1)], 1)
-    own = (mine + got.astype(F32) + beside.astype(F32)).astype(BF)
-    asked, own = after(asked, own)
+    candidates_in, mine = after(candidates, mine + beside.astype(F32))
+    asked = [lax.dynamic_index_in_dim(candidates_in, user ^ u, 0, False) for u in range(users)]
+    asked = asked[:1] + [swap(asked[u], u, "cand", users) for u in range(1, users)]
+    asked = jnp.concatenate(asked, 0)
+    asked = jnp.concatenate([asked, swap(asked, 1)], 0)
+    own = (mine + got.astype(F32)).astype(BF)
     step = SHARERS
     got = swap(own, step)
-    user = lax.axis_index("cand")
-    asked = [lax.dynamic_index_in_dim(asked, user ^ u, 0, False) for u in range(users)]
-    asked = asked[:1] + [swap(asked[u], u, "cand", users) for u in range(1, users)]
-    asked = jnp.stack(asked, 1).reshape(2 * users * candidates.shape[1], -1)
     while step * 2 < parts:
         step *= 2
         own = (own.astype(F32) + got.astype(F32)).astype(BF)
-        asked, own = after(asked, own)
+        asked, candidates_in, own = lax.optimization_barrier((asked, candidates_in, own))
         got = swap(own, step)
+    width = candidates.shape[2]
+    base = jnp.dot(
+        candidates_in.reshape(-1, width), w_hidden[:width], preferred_element_type=F32
+    )
+    base = base + b_hidden
     partial = attend(own, got, asked, swap(asked, 2), w_query, w_key, users, bits, digits)
     group = SHARERS * users
     groups = [[g * group + k for k in range(group)] for g in range(parts // SHARERS)]
     back = lax.all_to_all(partial, ("seq", "cand"), 0, 0, tiled=True, axis_index_groups=groups)
-    return rank(back, candidates, w_hidden, b_hidden, w_out)
+    return rank(back, base, w_hidden, w_out, users)
 
 
 def solution(mesh):

time: 38 us -> 40.1 us (1.055)
  blocking collectives: 7.34 us -> 0 us
  waiting for transfers between devices: 9.51 us -> 14.4 us
  starting transfers between devices: 11.3 us -> 14.9 us
  Pallas kernels: 8.75 us -> 9.34 us
    all_to_all x1 -> x0, blocking collectives: 7.34 us -> none  [on_device(): lax.all_to_all(partial, ('seq', 'cand'), 0, 0, tiled=True, axis_index_gro...]
    all_to_all x0 -> x1, waiting for transfers between devices: none -> 4.78 us  [on_device(): lax.all_to_all(partial, ('seq', 'cand'), 0, 0, tiled=True, axis_index_gro...]
    all_to_all x0 -> x1, starting transfers between devices: none -> 3.77 us  [on_device(): lax.all_to_all(partial, ('seq', 'cand'), 0, 0, tiled=True, axis_index_gro...]
    pallas_call x1, Pallas kernels: 0.64 us -> 1.3 us  [attend(): pl.pallas_call(functools.partial(attend_kernel, width, users, bits, digit...]
  transfers between devices with their start and end apart: 8 -> 9, of which waited for: 7 -> 8; matrix products, arithmetic and copies ran while one was open for 0% -> 1% of each run, Pallas kernels for 6% -> 6%
where the time goes in v3:
time: 40.1 us; the launch traced here: 39.7 us
  starting transfers between devices  14.9 us (37%)
  waiting for transfers between devices  14.4 us (36%)
  Pallas kernels  9.34 us (23%)
  between operations  0.79 us (2%)
    ppermute x8, starting transfers between devices, swap(): return lax.ppermute(value, axis, [(i, i ^ step) for i in range(count)])  11.1 us
    ppermute x8, waiting for transfers between devices, swap(): return lax.ppermute(value, axis, [(i, i ^ step) for i in range(count)])  9.57 us
    all_to_all x1, waiting for transfers between devices, on_device(): lax.all_to_all(partial, ('seq', 'cand'), 0, 0, tiled=True, axis_index_gro...  4.78 us
    pallas_call x1, Pallas kernels, pool_far(): pl.pallas_call(functools.partial(far_kernel, low, *plan), grid=(slots //...  4.6 us
    all_to_all x1, starting transfers between devices, on_device(): lax.all_to_all(partial, ('seq', 'cand'), 0, 0, tiled=True, axis_index_gro...  3.77 us
    pallas_call x1, Pallas kernels, pool_near(): pl.pallas_call(functools.partial(near_kernel, low, *plan, min(2048, slots...  2.45 us
    pallas_call x1, Pallas kernels, attend(): pl.pallas_call(functools.partial(attend_kernel, width, users, bits, digit...  1.3 us
    pallas_call x1, Pallas kernels, rank(): pl.pallas_call(functools.partial(rank_kernel, users), out_shape=jax.Shape...  0.98 us
  transfers between devices with their start and end apart: 9, of which 8 were waited for; matrix products, arithmetic and copies ran while one was open for 1% of the time, Pallas kernels for 6%

profile of v3, /device:TPU:0, one launch (start us, length us, event | category | flops | bytes accessed | tf_op | source)
XLA Modules:
  0.0 39.7 jit_solution(11411119176200850282)
XLA Ops:
  0.7 4.6 %pool_far.1 = (bf16[272,256]{1,0:T(8,128)(2,1)S(1)}, f32[272,256]{1,0:T(8,128)S(1)}, bf16[128,8192]{1,0:T(8,128)(2,1)S(1)}) custom-call(s32[1,1]{1,0:T(1,128)S(6)} %copy.10.live, s32[1,8192]{1,0:T(1,128)} %ids_ref.3, f32[8192,128]{1,0:T(8,128)} %bitcast.9), custom_call_target="tpu_custom_call" | custom-call | tf_op jit(solution)/shard_map/pool_far/pallas_call | solution.py:107
  5.3 0.5 %collective-permute-start = (bf16[272,256]{1,0:T(8,128)(2,1)S(1)}, bf16[272,256]{1,0:T(8,128)(2,1)S(1)}, u32[]{:S(2)}, u32[]{:S(2)}) collective-permute-start(bf16[272,256]{1,0:T(8,128)(2,1)S(1)} %get-tuple-element.18), channel_id=1, source_target_pairs={{0,2},{2,0},{4,6},{6,4},{8,10},{10,8},{12,14},{14,12},{16,18},{18,... | collective-permute-start | bytes 417800 | tf_op jit(solution)/shard_map/ppermute | solution.py:249
  5.8 1.0 %collective-permute-done = bf16[272,256]{1,0:T(8,128)(2,1)S(1)} collective-permute-done((bf16[272,256]{1,0:T(8,128)(2,1)S(1)}, bf16[272,256]{1,0:T(8,128)(2,1)S(1)}, u32[]{:S(2)}, u32[]{:S(2)}) %collective-permute-start) | collective-permute-done | bytes 139296 | tf_op jit(solution)/shard_map/ppermute | solution.py:249
  6.8 0.0 copy-start.5
  6.8 0.0 copy-start.2
  6.9 0.0 copy-start.3
  6.9 0.0 copy-start
  6.9 0.0 copy-start.6
  6.9 0.0 copy-start.4
  6.9 2.9 %collective-permute-start.1 = (bf16[272,256]{1,0:T(8,128)(2,1)S(1)}, bf16[272,256]{1,0:T(8,128)(2,1)S(1)}, u32[]{:S(2)}, u32[]{:S(2)}) collective-permute-start(bf16[272,256]{1,0:T(8,128)(2,1)S(1)} %add_convert_fusion.2), channel_id=1, source_target_pairs={{0,4},{2,6},{4,0},{6,2},{8,12},{10,14},{12,8},{14,10},{16,20},{18,... | collective-permute-start | bytes 417800 | tf_op jit(solution)/shard_map/ppermute | solution.py:249
  9.8 0.0 copy-done.1
  9.8 2.5 %pool_near.1 = (bf16[272,256]{1,0:T(8,128)(2,1)S(1)}, f32[272,256]{1,0:T(8,128)S(1)}) custom-call(s32[1,1]{1,0:T(1,128)S(6)} %copy.10.live, s32[1,8192]{1,0:T(1,128)S(1)} %copy-done.1, bf16[128,8192]{1,0:T(8,128)(2,1)S(1)} %get-tuple-element.19.turned_ref), custom_call_target="tpu_custom_call" | custom-call | flops 2214592512 | bytes 2097152 | tf_op jit(solution)/shard_map/pool_near/pallas_call | solution.py:139
  12.3 0.1 collective-permute-start.4
  12.4 1.4 %collective-permute-done.1 = bf16[272,256]{1,0:T(8,128)(2,1)S(1)} collective-permute-done((bf16[272,256]{1,0:T(8,128)(2,1)S(1)}, bf16[272,256]{1,0:T(8,128)(2,1)S(1)}, u32[]{:S(2)}, u32[]{:S(2)}) %collective-permute-start.1) | collective-permute-done | bytes 139296 | tf_op jit(solution)/shard_map/ppermute | solution.py:249
  13.8 0.0 copy-done.5
  13.9 1.8 %collective-permute-start.2 = (bf16[32,128]{1,0:T(8,128)(2,1)S(1)}, bf16[32,128]{1,0:T(8,128)(2,1)S(1)}, u32[]{:S(2)}, u32[]{:S(2)}) collective-permute-start(bf16[32,128]{1,0:T(8,128)(2,1)S(1)} %get-tuple-element.30), channel_id=1, source_target_pairs={{0,1},{1,0},{2,3},{3,2},{4,5},{5,4},{6,7},{7,6},{8,9},{9,8},{10,11... | collective-permute-start | bytes 24584 | tf_op jit(solution)/shard_map/ppermute | solution.py:249
  15.7 0.0 collective-permute-done.4
  15.7 1.6 %collective-permute-start.5 = (bf16[272,256]{1,0:T(8,128)(2,1)S(1)}, bf16[272,256]{1,0:T(8,128)(2,1)S(1)}, u32[]{:S(2)}, u32[]{:S(2)}) collective-permute-start(bf16[272,256]{1,0:T(8,128)(2,1)S(1)} %add_convert_fusion.1), channel_id=1, source_target_pairs={{0,8},{2,10},{4,12},{6,14},{8,0},{10,2},{12,4},{14,6},{16,24},{18,... | collective-permute-start | bytes 417800 | tf_op jit(solution)/shard_map/ppermute | solution.py:249
  17.4 0.2 collective-permute-done.2
  17.6 0.0 collective-permute-start.3
  17.6 1.2 %collective-permute-done.3 = bf16[64,128]{1,0:T(8,128)(2,1)S(1)} collective-permute-done((bf16[64,128]{1,0:T(8,128)(2,1)S(1)}, bf16[64,128]{1,0:T(8,128)(2,1)S(1)}, u32[]{:S(2)}, u32[]{:S(2)}) %collective-permute-start.3) | collective-permute-done | bytes 16416 | tf_op jit(solution)/shard_map/ppermute | solution.py:249
  18.8 2.1 %collective-permute-done.5 = bf16[272,256]{1,0:T(8,128)(2,1)S(1)} collective-permute-done((bf16[272,256]{1,0:T(8,128)(2,1)S(1)}, bf16[272,256]{1,0:T(8,128)(2,1)S(1)}, u32[]{:S(2)}, u32[]{:S(2)}) %collective-permute-start.5) | collective-permute-done | bytes 139296 | tf_op jit(solution)/shard_map/ppermute | solution.py:249
  20.9 2.7 %collective-permute-start.6 = (bf16[272,256]{1,0:T(8,128)(2,1)S(1)}, bf16[272,256]{1,0:T(8,128)(2,1)S(1)}, u32[]{:S(2)}, u32[]{:S(2)}) collective-permute-start(bf16[272,256]{1,0:T(8,128)(2,1)S(1)} %add_convert_fusion.own_ref), channel_id=1, source_target_pairs={{0,16},{2,18},{4,20},{6,22},{8,24},{10,26},{12,28},{14,30},{16,0},... | collective-permute-start | bytes 417800 | tf_op jit(solution)/shard_map/ppermute | solution.py:249
  23.5 1.5 %collective-permute-start.7 = (bf16[128,128]{1,0:T(8,128)(2,1)S(1)}, bf16[128,128]{1,0:T(8,128)(2,1)S(1)}, u32[]{:S(2)}, u32[]{:S(2)}) collective-permute-start(bf16[128,128]{1,0:T(8,128)(2,1)S(1)} %pad_maximum_fusion.cand_ref), channel_id=1, source_target_pairs={{0,4},{2,6},{4,0},{6,2},{8,12},{10,14},{12,8},{14,10},{16,20},{18,... | collective-permute-start | bytes 98312 | tf_op jit(solution)/shard_map/ppermute | solution.py:249
  25.0 2.4 %collective-permute-done.7.other_ref = bf16[128,128]{1,0:T(8,128)(2,1)S(1)} collective-permute-done((bf16[128,128]{1,0:T(8,128)(2,1)S(1)}, bf16[128,128]{1,0:T(8,128)(2,1)S(1)}, u32[]{:S(2)}, u32[]{:S(2)}) %collective-permute-start.7) | collective-permute-done | bytes 32800 | tf_op jit(solution)/shard_map/ppermute | solution.py:249
  27.5 1.2 %collective-permute-done.6.got_ref = bf16[272,256]{1,0:T(8,128)(2,1)S(1)} collective-permute-done((bf16[272,256]{1,0:T(8,128)(2,1)S(1)}, bf16[272,256]{1,0:T(8,128)(2,1)S(1)}, u32[]{:S(2)}, u32[]{:S(2)}) %collective-permute-start.6) | collective-permute-done | bytes 139296 | tf_op jit(solution)/shard_map/ppermute | solution.py:249
  28.7 1.3 %attend.1 = bf16[8,32,256]{2,1,0:T(8,128)(2,1)} custom-call(bf16[272,256]{1,0:T(8,128)(2,1)S(1)} %add_convert_fusion.own_ref, bf16[272,256]{1,0:T(8,128)(2,1)S(1)} %collective-permute-done.6.got_ref, bf16[128,128]{1,0:T(8,128)(2,1)S(1)} %pad_maximum_fusion.cand_ref, bf16[128,128]{1,0:T(8,128)(2,1)S(1)} %collective-permute-done.7.other_ref, ...), custom_call_target="tpu_custom_call" | custom-call | tf_op jit(solution)/shard_map/attend/pallas_call | solution.py:199
  30.0 3.8 %all-to-all-start = ((bf16[8,32,256]{2,1,0:T(8,128)(2,1)}), bf16[8,32,256]{2,1,0:T(8,128)(2,1)S(1)}, u32[]{:S(2)}, u32[]{:S(2)}) async-start(bf16[8,32,256]{2,1,0:T(8,128)(2,1)} %attend.1), calls=%async_computation | async-start | bytes 262144 | tf_op jit(solution)/shard_map/all_to_all | solution.py:282
  33.8 0.1 convolution_add_fusion.base_ref
  33.9 4.8 %all-to-all-done.got_ref = bf16[8,32,256]{2,1,0:T(8,128)(2,1)S(1)} async-done(((bf16[8,32,256]{2,1,0:T(8,128)(2,1)}), bf16[8,32,256]{2,1,0:T(8,128)(2,1)S(1)}, u32[]{:S(2)}, u32[]{:S(2)}) %all-to-all-start) | async-done | bytes 131104 | tf_op jit(solution)/shard_map/all_to_all | solution.py:282
  38.7 0.0 copy-done.4
  38.7 1.0 %rank.1 = f32[2,32]{1,0:T(2,128)} custom-call(bf16[8,32,256]{2,1,0:T(8,128)(2,1)S(1)} %all-to-all-done.got_ref, f32[64,512]{1,0:T(8,128)S(1)} %convolution_add_fusion.base_ref, bf16[256,512]{1,0:T(8,128)(2,1)S(1)} %copy-done, f32[1,512]{1,0:T(1,128)S(1)} %bitcast.8), custom_call_target="tpu_custom_call" | custom-call | tf_op jit(solution)/shard_map/rank/pallas_call | solution.py:235
  (12 shorter events, 0.2 us)
Async XLA Ops:
  0.0 9.8 %copy-start.1 = (s32[1,8192]{1,0:T(1,128)S(1)}, s32[1,8192]{1,0:T(1,128)}, u32[]{:S(2)}) copy-start(s32[1,8192]{1,0:T(1,128)} %ids_ref.3) | copy-start | bytes 98308
  5.3 1.5 %collective-permute-start = (bf16[272,256]{1,0:T(8,128)(2,1)S(1)}, bf16[272,256]{1,0:T(8,128)(2,1)S(1)}, u32[]{:S(2)}, u32[]{:S(2)}) collective-permute-start(bf16[272,256]{1,0:T(8,128)(2,1)S(1)} %get-tuple-element.18), channel_id=1, source_target_pairs={{0,2},{2,0},{4,6},{6,4},{8,10},{10,8},{12,14},{14,12},{16,18},{18,... | collective-permute-start | bytes 417800 | tf_op jit(solution)/shard_map/ppermute | solution.py:249
  6.8 7.0 %copy-start.5 = (bf16[2,32,128]{2,1,0:T(8,128)(2,1)S(1)}, bf16[2,32,128]{2,1,0:T(8,128)(2,1)}, u32[]{:S(2)}) copy-start(bf16[2,32,128]{2,1,0:T(8,128)(2,1)} %param.12) | copy-start | bytes 49156
  6.8 21.9 %copy-start.2 = (bf16[128,128]{1,0:T(8,128)(2,1)S(1)}, bf16[128,128]{1,0:T(8,128)(2,1)}, u32[]{:S(2)}) copy-start(bf16[128,128]{1,0:T(8,128)(2,1)} %wq_ref.1) | copy-start | bytes 98308
  6.9 21.9 %copy-start.3 = (bf16[128,128]{1,0:T(8,128)(2,1)S(1)}, bf16[128,128]{1,0:T(8,128)(2,1)}, u32[]{:S(2)}) copy-start(bf16[128,128]{1,0:T(8,128)(2,1)} %wk_ref.1) | copy-start | bytes 98308
  6.9 26.9 %copy-start = (bf16[256,512]{1,0:T(8,128)(2,1)S(1)}, bf16[256,512]{1,0:T(8,128)(2,1)}, u32[]{:S(2)}) copy-start(bf16[256,512]{1,0:T(8,128)(2,1)} %wh_ref.1) | copy-start | bytes 786436
  6.9 26.9 %copy-start.6 = (f32[512]{0:T(512)S(1)}, f32[512]{0:T(512)}, u32[]{:S(2)}) copy-start(f32[512]{0:T(512)} %param.16) | copy-start | bytes 6148
  6.9 31.8 %copy-start.4 = (f32[512]{0:T(512)S(1)}, f32[512]{0:T(512)}, u32[]{:S(2)}) copy-start(f32[512]{0:T(512)} %param.17) | copy-start | bytes 6148
  6.9 6.9 %collective-permute-start.1 = (bf16[272,256]{1,0:T(8,128)(2,1)S(1)}, bf16[272,256]{1,0:T(8,128)(2,1)S(1)}, u32[]{:S(2)}, u32[]{:S(2)}) collective-permute-start(bf16[272,256]{1,0:T(8,128)(2,1)S(1)} %add_convert_fusion.2), channel_id=1, source_target_pairs={{0,4},{2,6},{4,0},{6,2},{8,12},{10,14},{12,8},{14,10},{16,20},{18,... | collective-permute-start | bytes 417800 | tf_op jit(solution)/shard_map/ppermute | solution.py:249
  12.3 3.4 %collective-permute-start.4 = (bf16[272,256]{1,0:T(8,128)(2,1)S(1)}, bf16[272,256]{1,0:T(8,128)(2,1)S(1)}, u32[]{:S(2)}, u32[]{:S(2)}) collective-permute-start(bf16[272,256]{1,0:T(8,128)(2,1)S(1)} %get-tuple-element.25), channel_id=1, source_target_pairs={{0,2},{2,0},{4,6},{6,4},{8,10},{10,8},{12,14},{14,12},{16,18},{18,... | collective-permute-start | bytes 417800 | tf_op jit(solution)/shard_map/ppermute | solution.py:249
  13.9 3.7 %collective-permute-start.2 = (bf16[32,128]{1,0:T(8,128)(2,1)S(1)}, bf16[32,128]{1,0:T(8,128)(2,1)S(1)}, u32[]{:S(2)}, u32[]{:S(2)}) collective-permute-start(bf16[32,128]{1,0:T(8,128)(2,1)S(1)} %get-tuple-element.30), channel_id=1, source_target_pairs={{0,1},{1,0},{2,3},{3,2},{4,5},{5,4},{6,7},{7,6},{8,9},{9,8},{10,11... | collective-permute-start | bytes 24584 | tf_op jit(solution)/shard_map/ppermute | solution.py:249
  15.7 5.1 %collective-permute-start.5 = (bf16[272,256]{1,0:T(8,128)(2,1)S(1)}, bf16[272,256]{1,0:T(8,128)(2,1)S(1)}, u32[]{:S(2)}, u32[]{:S(2)}) collective-permute-start(bf16[272,256]{1,0:T(8,128)(2,1)S(1)} %add_convert_fusion.1), channel_id=1, source_target_pairs={{0,8},{2,10},{4,12},{6,14},{8,0},{10,2},{12,4},{14,6},{16,24},{18,... | collective-permute-start | bytes 417800 | tf_op jit(solution)/shard_map/ppermute | solution.py:249
  17.6 1.2 %collective-permute-start.3 = (bf16[64,128]{1,0:T(8,128)(2,1)S(1)}, bf16[64,128]{1,0:T(8,128)(2,1)S(1)}, u32[]{:S(2)}, u32[]{:S(2)}) collective-permute-start(bf16[64,128]{1,0:T(8,128)(2,1)S(1)} %pad_maximum_fusion.1), channel_id=1, source_target_pairs={{0,2},{2,0},{4,6},{6,4},{8,10},{10,8},{12,14},{14,12},{16,18},{18,... | collective-permute-start | bytes 49160 | tf_op jit(solution)/shard_map/ppermute | solution.py:249
  20.9 7.8 %collective-permute-start.6 = (bf16[272,256]{1,0:T(8,128)(2,1)S(1)}, bf16[272,256]{1,0:T(8,128)(2,1)S(1)}, u32[]{:S(2)}, u32[]{:S(2)}) collective-permute-start(bf16[272,256]{1,0:T(8,128)(2,1)S(1)} %add_convert_fusion.own_ref), channel_id=1, source_target_pairs={{0,16},{2,18},{4,20},{6,22},{8,24},{10,26},{12,28},{14,30},{16,0},... | collective-permute-start | bytes 417800 | tf_op jit(solution)/shard_map/ppermute | solution.py:249
  23.5 3.9 %collective-permute-start.7 = (bf16[128,128]{1,0:T(8,128)(2,1)S(1)}, bf16[128,128]{1,0:T(8,128)(2,1)S(1)}, u32[]{:S(2)}, u32[]{:S(2)}) collective-permute-start(bf16[128,128]{1,0:T(8,128)(2,1)S(1)} %pad_maximum_fusion.cand_ref), channel_id=1, source_target_pairs={{0,4},{2,6},{4,0},{6,2},{8,12},{10,14},{12,8},{14,10},{16,20},{18,... | collective-permute-start | bytes 98312 | tf_op jit(solution)/shard_map/ppermute | solution.py:249
  30.0 8.7 %all-to-all-start = ((bf16[8,32,256]{2,1,0:T(8,128)(2,1)}), bf16[8,32,256]{2,1,0:T(8,128)(2,1)S(1)}, u32[]{:S(2)}, u32[]{:S(2)}) async-start(bf16[8,32,256]{2,1,0:T(8,128)(2,1)} %attend.1), calls=%async_computation | async-start | bytes 262144 | tf_op jit(solution)/shard_map/all_to_all | solution.py:282

commit v4 on v3

--- a/solution.py
+++ b/solution.py
@@ -12,6 +12,8 @@
 F32 = jnp.float32
 PAD = 16
 SHARERS = 4
+FIRST_BLOCK = 4096
+NEXT_BLOCK = 2048
 NT = (((1,), (1,)), ((), ()))
 TN = (((0,), (0,)), ((), ()))
 NN = (((1,), (0,)), ((), ()))
@@ -24,11 +26,9 @@
     return bits, -(-(slots.bit_length()) // bits)
 
 
-def split(ids, slots_before, live, flip, first, low):
-    slot = slots_before + lax.broadcasted_iota(jnp.int32, ids.shape, 1)
-    high = ((ids >> (low.bit_length() - 1)) ^ flip) - first
-    high = jnp.where(slot < live, high, -PAD)
-    return high.astype(F32).astype(BF), (ids & (low - 1)).astype(F32).astype(BF)
+def split(marked, first, low):
+    high = (marked >> (low.bit_length() - 1)) - first
+    return high.astype(F32).astype(BF), (marked & (low - 1)).astype(F32).astype(BF)
 
 
 def labels(count):
@@ -61,13 +61,18 @@
     return (place & 1) * 2 + (place & 2) * 2
 
 
-def far_kernel(low, bits, digits, live, ids_ref, rows_ref, send_ref, keep_ref, turned_ref, total):
+def first_kernel(
+    low, bits, digits, live_ref, ids_ref, rows_ref, send_ref, turned_ref, marked_ref, total
+):
     step, steps = pl.program_id(0), pl.num_programs(0)
     block, width = rows_ref.shape
     turned = jnp.transpose(rows_ref[...].astype(BF))
     turned_ref[...] = turned
-    high, within = split(ids_ref[...], step * block, live[0, 0], flip_of("seq"), SHARERS, low)
-    part = pooled(turned, high, within, low, SHARERS)
+    slot = step * block + lax.broadcasted_iota(jnp.int32, ids_ref.shape, 1)
+    marked = jnp.where(slot < live_ref[0, 0], ids_ref[...] ^ (flip_of("seq") * low), -1)
+    marked_ref[...] = marked
+    high, within = split(marked, 2 * SHARERS - 2, low)
+    part = pooled(turned, high, within, low, 2)
 
     @pl.when(step == 0)
     def _():
@@ -79,33 +84,33 @@
 
     @pl.when(step == steps - 1)
     def _():
-        give(total[...], width, bits, digits, (keep_ref, send_ref))
-
-
-def near_kernel(low, bits, digits, block, live, ids_ref, turned_ref, send_ref, keep_ref, total):
+        give(total[...], width, bits, digits, (send_ref,))
+
+
+def next_kernel(low, bits, digits, block, first, marked_ref, turned_ref, *refs):
+    dests, total = refs[:-1], refs[-1]
     width, slots = turned_ref.shape
     for start in range(0, slots, block):
         there = slice(start, start + block)
-        high, within = split(ids_ref[:, there], start, live[0, 0], flip_of("seq"), 0, low)
-        part = pooled(turned_ref[:, there], high, within, low, SHARERS)
+        high, within = split(marked_ref[:, there], first, low)
+        part = pooled(turned_ref[:, there], high, within, low, 2 * len(dests))
         if start == 0:
             total[...] = part
         else:
             total[...] += part
-    give(total[...], width, bits, digits, (keep_ref, send_ref))
+    give(total[...], width, bits, digits, dests)
 
 
 def sizes(slots, width, parts):
-    low = CLUSTERS // (2 * SHARERS)
-    return low, SHARERS * width + PAD, 2 * width + PAD, digit_plan(parts, slots)
-
-
-def pool_far(rows, ids, lengths, parts):
+    return CLUSTERS // (2 * SHARERS), 2 * width + PAD, digit_plan(parts, slots)
+
+
+def pool_first(rows, ids, lengths, parts):
     slots, width = rows.shape
-    low, tall, height, plan = sizes(slots, width, parts)
-    block = min(4096, slots)
+    low, height, plan = sizes(slots, width, parts)
+    block = min(FIRST_BLOCK, slots)
     return pl.pallas_call(
-        functools.partial(far_kernel, low, *plan),
+        functools.partial(first_kernel, low, *plan),
         grid=(slots // block,),
         in_specs=[
             pl.BlockSpec(memory_space=pltpu.SMEM),
@@ -114,43 +119,34 @@
         ],
         out_specs=[
             pl.BlockSpec((height, low), lambda b: (0, 0)),
-            pl.BlockSpec((height, low), lambda b: (0, 0)),
             pl.BlockSpec((width, block), lambda b: (0, b)),
+            pl.BlockSpec((1, block), lambda b: (0, b)),
         ],
         out_shape=[
             jax.ShapeDtypeStruct((height, low), BF),
-            jax.ShapeDtypeStruct((height, low), F32),
             jax.ShapeDtypeStruct((width, slots), BF),
+            jax.ShapeDtypeStruct((1, slots), jnp.int32),
         ],
+        scratch_shapes=[pltpu.VMEM((height, low), F32)],
+        compiler_params=pltpu.CompilerParams(vmem_limit_bytes=44 << 20),
+        name="pool_first",
+    )(lengths, *(pltpu.with_memory_space_constraint(v, pltpu.HBM) for v in (ids, rows)))
+
+
+def pool_next(turned, marked, first, types, parts):
+    width, slots = turned.shape
+    low, height, plan = sizes(slots, width, parts)
+    vmem = pl.BlockSpec(memory_space=pltpu.VMEM)
+    tall = 2 * len(types) * width + PAD
+    return pl.pallas_call(
+        functools.partial(next_kernel, low, *plan, min(NEXT_BLOCK, slots), first),
+        in_specs=[vmem, vmem],
+        out_specs=[vmem] * len(types),
+        out_shape=[jax.ShapeDtypeStruct((height, low), t) for t in types],
         scratch_shapes=[pltpu.VMEM((tall, low), F32)],
         compiler_params=pltpu.CompilerParams(vmem_limit_bytes=44 << 20),
-        name="pool_far",
-    )(
-        lengths,
-        pltpu.with_memory_space_constraint(ids, pltpu.HBM),
-        pltpu.with_memory_space_constraint(rows, pltpu.HBM),
-    )
-
-
-def pool_near(turned, ids, lengths, parts):
-    width, slots = turned.shape
-    low, tall, height, plan = sizes(slots, width, parts)
-    vmem = pl.BlockSpec(memory_space=pltpu.VMEM)
-    return pl.pallas_call(
-        functools.partial(near_kernel, low, *plan, min(2048, slots)),
-        in_specs=[pl.BlockSpec(memory_space=pltpu.SMEM), vmem, vmem],
-        out_specs=[vmem, vmem],
-        out_shape=[
-            jax.ShapeDtypeStruct((height, low), BF),
-            jax.ShapeDtypeStruct((height, low), F32),
-        ],
-        scratch_shapes=[pltpu.VMEM((tall, low), F32)],
-        compiler_params=pltpu.CompilerParams(vmem_limit_bytes=44 << 20),
-        cost_estimate=pl.CostEstimate(
-            flops=2 * tall * low * slots, bytes_accessed=2 * width * slots, transcendentals=0
-        ),
-        name="pool_near",
-    )(lengths, ids, turned)
+        name="pool_next",
+    )(marked, turned)
 
 
 def attend_kernel(width, users, bits, digits, own_ref, got_ref, cand_ref, other_ref, wq_ref, wk_ref, out_ref):
@@ -251,31 +247,32 @@
     def after(value, earlier):
         return lax.optimization_barrier((value, earlier))
 
-    user = lax.axis_index("cand")
-    send, beyond, turned = pool_far(behaviors[0], cluster_ids, lengths, parts)
+    send, turned, marked = pool_first(behaviors[0], cluster_ids, lengths, parts)
     got = swap(send, 1)
+    (beyond,) = pool_next(turned, marked, SHARERS, [F32], parts)
     turned, got = after(turned, got)
     beside = swap((beyond + got.astype(F32)).astype(BF), 2)
-    send, mine = pool_near(turned, cluster_ids, lengths, parts)
+    mine, send = pool_next(turned, marked, 0, [F32, BF], parts)
+    candidates_in, send = after(candidates, send)
     got = swap(send, 1)
-    candidates_in, mine = after(candidates, mine + beside.astype(F32))
-    asked = [lax.dynamic_index_in_dim(candidates_in, user ^ u, 0, False) for u in range(users)]
-    asked = asked[:1] + [swap(asked[u], u, "cand", users) for u in range(1, users)]
-    asked = jnp.concatenate(asked, 0)
-    asked = jnp.concatenate([asked, swap(asked, 1)], 0)
-    own = (mine + got.astype(F32)).astype(BF)
+    asked = jnp.stack([candidates_in, swap(candidates_in, 1)], 1)
+    own = (mine + got.astype(F32) + beside.astype(F32)).astype(BF)
+    asked, own = after(asked, own)
     step = SHARERS
     got = swap(own, step)
+    user = lax.axis_index("cand")
+    asked = [lax.dynamic_index_in_dim(asked, user ^ u, 0, False) for u in range(users)]
+    asked = asked[:1] + [swap(asked[u], u, "cand", users) for u in range(1, users)]
+    asked = jnp.stack(asked, 1).reshape(2 * users * candidates.shape[1], -1)
     while step * 2 < parts:
         step *= 2
         own = (own.astype(F32) + got.astype(F32)).astype(BF)
-        asked, candidates_in, own = lax.optimization_barrier((asked, candidates_in, own))
+        asked, candidates_late, own = lax.optimization_barrier((asked, candidates, own))
         got = swap(own, step)
     width = candidates.shape[2]
-    base = jnp.dot(
-        candidates_in.reshape(-1, width), w_hidden[:width], preferred_element_type=F32
-    )
-    base = base + b_hidden
+    rows = candidates_late.reshape(-1, width)
+    base = jnp.dot(rows, w_hidden[:width], preferred_element_type=F32) + b_hidden
+    base, got = after(base, got)
     partial = attend(own, got, asked, swap(asked, 2), w_query, w_key, users, bits, digits)
     group = SHARERS * users
     groups = [[g * group + k for k in range(group)] for g in range(parts // SHARERS)]

time: 40.1 us -> 37.4 us (0.933)
  blocking collectives: 0 us -> 8.26 us
  waiting for transfers between devices: 14.4 us -> 7.73 us
  starting transfers between devices: 14.9 us -> 11.2 us
    all_to_all x0 -> x1, blocking collectives: none -> 8.26 us  [on_device(): lax.all_to_all(partial, ('seq', 'cand'), 0, 0, tiled=True, axis_index_gro...]
    all_to_all x1 -> x0, waiting for transfers between devices: 4.78 us -> none  [on_device(): lax.all_to_all(partial, ('seq', 'cand'), 0, 0, tiled=True, axis_index_gro...]
    all_to_all x1 -> x0, starting transfers between devices: 3.77 us -> none  [on_device(): lax.all_to_all(partial, ('seq', 'cand'), 0, 0, tiled=True, axis_index_gro...]
    ppermute x8, waiting for transfers between devices: 9.57 us -> 7.73 us  [swap(): return lax.ppermute(value, axis, [(i, i ^ step) for i in range(count)])]
    pallas_call x1, Pallas kernels: 1.3 us -> 0.64 us  [attend(): pl.pallas_call(functools.partial(attend_kernel, width, users, bits, digit...]
    pallas_call x2 -> x3, Pallas kernels: 7.06 us -> 7.34 us  [the longest x2 3.83 us: pool_next(): pl.pallas_call(functools.partial(next_kernel, low, *plan, min(NEXT_BLOCK,...]
  transfers between devices with their start and end apart: 9 -> 8, of which waited for: 8 -> 4; matrix products, arithmetic and copies ran while one was open for 1% -> 0% of each run, Pallas kernels for 6% -> 10%
where the time goes in v4:
time: 37.4 us; the launch traced here: 37.3 us
  starting transfers between devices  11.2 us (30%)
  Pallas kernels  8.96 us (24%)
  blocking collectives  8.26 us (22%)
  waiting for transfers between devices  7.73 us (21%)
  between operations  0.78 us (2%)
    ppermute x8, starting transfers between devices, swap(): return lax.ppermute(value, axis, [(i, i ^ step) for i in range(count)])  11.2 us
    all_to_all x1, blocking collectives, on_device(): lax.all_to_all(partial, ('seq', 'cand'), 0, 0, tiled=True, axis_index_gro...  8.26 us
    ppermute x8, waiting for transfers between devices, swap(): return lax.ppermute(value, axis, [(i, i ^ step) for i in range(count)])  7.73 us
    pallas_call x2, Pallas kernels, pool_next(): pl.pallas_call(functools.partial(next_kernel, low, *plan, min(NEXT_BLOCK,...  3.83 us
    pallas_call x1, Pallas kernels, pool_first(): pl.pallas_call(functools.partial(first_kernel, low, *plan), grid=(slots /...  3.51 us
    pallas_call x1, Pallas kernels, rank(): pl.pallas_call(functools.partial(rank_kernel, users), out_shape=jax.Shape...  0.98 us
  transfers between devices with their start and end apart: 8, of which 4 were waited for; matrix products, arithmetic and copies ran while one was open for 0% of the time, Pallas kernels for 10%

profile of v4, /device:TPU:0, one launch (start us, length us, event | category | flops | bytes accessed | tf_op | source)
XLA Modules:
  0.0 37.3 jit_solution(1520185208583743014)
XLA Ops:
  0.7 0.0 copy-start.4
  0.7 3.5 %pool_first.1 = (bf16[272,256]{1,0:T(8,128)(2,1)S(1)}, bf16[128,8192]{1,0:T(8,128)(2,1)S(1)}, s32[1,8192]{1,0:T(1,128)S(1)}) custom-call(s32[1,1]{1,0:T(1,128)S(6)} %copy.10.live_ref, s32[1,8192]{1,0:T(1,128)} %ids_ref.1, f32[8192,128]{1,0:T(8,128)} %bitcast.15), custom_call_target="tpu_custom_call" | custom-call | tf_op jit(solution)/shard_map/pool_first/pallas_call | solution.py:112
  4.2 0.0 copy-start
  4.2 0.0 copy-start.5
  4.2 0.0 copy-start.1
  4.2 0.0 copy-start.2
  4.2 0.0 copy-start.3
  4.2 0.5 %collective-permute-start = (bf16[272,256]{1,0:T(8,128)(2,1)S(1)}, bf16[272,256]{1,0:T(8,128)(2,1)S(1)}, u32[]{:S(2)}, u32[]{:S(2)}) collective-permute-start(bf16[272,256]{1,0:T(8,128)(2,1)S(1)} %get-tuple-element.23), channel_id=1, source_target_pairs={{0,2},{2,0},{4,6},{6,4},{8,10},{10,8},{12,14},{14,12},{16,18},{18,... | collective-permute-start | bytes 417800 | tf_op jit(solution)/shard_map/ppermute | solution.py:245
  4.8 1.4 %pool_next.3 = f32[272,256]{1,0:T(8,128)S(1)} custom-call(s32[1,8192]{1,0:T(1,128)S(1)} %get-tuple-element.21.marked_ref, bf16[128,8192]{1,0:T(8,128)(2,1)S(1)} %get-tuple-element.24.turned_ref), custom_call_target="tpu_custom_call" | custom-call | tf_op jit(solution)/shard_map/pool_next/pallas_call | solution.py:141
  6.1 0.0 collective-permute-done
  6.2 2.6 %collective-permute-start.3 = (bf16[272,256]{1,0:T(8,128)(2,1)S(1)}, bf16[272,256]{1,0:T(8,128)(2,1)S(1)}, u32[]{:S(2)}, u32[]{:S(2)}) collective-permute-start(bf16[272,256]{1,0:T(8,128)(2,1)S(1)} %add_convert_fusion.2), channel_id=1, source_target_pairs={{0,4},{2,6},{4,0},{6,2},{8,12},{10,14},{12,8},{14,10},{16,20},{18,... | collective-permute-start | bytes 417800 | tf_op jit(solution)/shard_map/ppermute | solution.py:245
  8.7 2.5 %pool_next.2 = (f32[272,256]{1,0:T(8,128)S(1)}, bf16[272,256]{1,0:T(8,128)(2,1)S(1)}) custom-call(s32[1,8192]{1,0:T(1,128)S(1)} %get-tuple-element.21.marked_ref, bf16[128,8192]{1,0:T(8,128)(2,1)S(1)} %get-tuple-element.24.turned_ref), custom_call_target="tpu_custom_call" | custom-call | tf_op jit(solution)/shard_map/pool_next/pallas_call | solution.py:141
  11.2 0.3 collective-permute-start.2
  11.5 0.0 copy-done.4
  11.5 0.3 collective-permute-start.1
  11.8 0.9 %collective-permute-done.1 = bf16[2,32,128]{2,1,0:T(8,128)(2,1)S(1)} collective-permute-done((bf16[2,32,128]{2,1,0:T(8,128)(2,1)S(1)}, bf16[2,32,128]{2,1,0:T(8,128)(2,1)S(1)}, u32[]{:S(2)}, u32[]{:S(2)}) %collective-permute-start.1) | collective-permute-done | bytes 16416 | tf_op jit(solution)/shard_map/ppermute | solution.py:245
  12.7 0.4 %collective-permute-done.3 = bf16[272,256]{1,0:T(8,128)(2,1)S(1)} collective-permute-done((bf16[272,256]{1,0:T(8,128)(2,1)S(1)}, bf16[272,256]{1,0:T(8,128)(2,1)S(1)}, u32[]{:S(2)}, u32[]{:S(2)}) %collective-permute-start.3) | collective-permute-done | bytes 139296 | tf_op jit(solution)/shard_map/ppermute | solution.py:245
  13.1 0.0 collective-permute-done.2
  13.1 0.1 add_convert_fusion.1
  13.2 1.9 %collective-permute-start.5 = (bf16[272,256]{1,0:T(8,128)(2,1)S(1)}, bf16[272,256]{1,0:T(8,128)(2,1)S(1)}, u32[]{:S(2)}, u32[]{:S(2)}) collective-permute-start(bf16[272,256]{1,0:T(8,128)(2,1)S(1)} %add_convert_fusion.1), channel_id=1, source_target_pairs={{0,8},{2,10},{4,12},{6,14},{8,0},{10,2},{12,4},{14,6},{16,24},{18,... | collective-permute-start | bytes 417800 | tf_op jit(solution)/shard_map/ppermute | solution.py:245
  15.1 1.5 %collective-permute-start.4 = (bf16[2,32,128]{2,1,0:T(8,128)(2,1)S(1)}, bf16[2,32,128]{2,1,0:T(8,128)(2,1)S(1)}, u32[]{:S(2)}, u32[]{:S(2)}) collective-permute-start(bf16[2,32,128]{2,1,0:T(8,128)(2,1)S(1)} %get-tuple-element.38), channel_id=1, source_target_pairs={{0,1},{1,0},{2,3},{3,2},{4,5},{5,4},{6,7},{7,6},{8,9},{9,8},{10,11... | collective-permute-start | bytes 49160 | tf_op jit(solution)/shard_map/ppermute | solution.py:245
  16.6 2.2 %collective-permute-done.4 = bf16[2,32,128]{2,1,0:T(8,128)(2,1)S(1)} collective-permute-done((bf16[2,32,128]{2,1,0:T(8,128)(2,1)S(1)}, bf16[2,32,128]{2,1,0:T(8,128)(2,1)S(1)}, u32[]{:S(2)}, u32[]{:S(2)}) %collective-permute-start.4) | collective-permute-done | bytes 16416 | tf_op jit(solution)/shard_map/ppermute | solution.py:245
  18.8 0.0 collective-permute-done.5
  18.8 2.7 %collective-permute-start.6 = (bf16[272,256]{1,0:T(8,128)(2,1)S(1)}, bf16[272,256]{1,0:T(8,128)(2,1)S(1)}, u32[]{:S(2)}, u32[]{:S(2)}) collective-permute-start(bf16[272,256]{1,0:T(8,128)(2,1)S(1)} %add_convert_fusion.own_ref), channel_id=1, source_target_pairs={{0,16},{2,18},{4,20},{6,22},{8,24},{10,26},{12,28},{14,30},{16,0},... | collective-permute-start | bytes 417800 | tf_op jit(solution)/shard_map/ppermute | solution.py:245
  21.5 1.5 %collective-permute-start.7 = (bf16[128,128]{1,0:T(8,128)(2,1)S(1)}, bf16[128,128]{1,0:T(8,128)(2,1)S(1)}, u32[]{:S(2)}, u32[]{:S(2)}) collective-permute-start(bf16[128,128]{1,0:T(8,128)(2,1)S(1)} %bitcast.12), channel_id=1, source_target_pairs={{0,4},{2,6},{4,0},{6,2},{8,12},{10,14},{12,8},{14,10},{16,20},{18,... | collective-permute-start | bytes 98312 | tf_op jit(solution)/shard_map/ppermute | solution.py:245
  23.0 0.0 copy-done
  23.0 0.1 convolution_add_fusion.base_ref
  23.1 4.2 %collective-permute-done.6.got_ref = bf16[272,256]{1,0:T(8,128)(2,1)S(1)} collective-permute-done((bf16[272,256]{1,0:T(8,128)(2,1)S(1)}, bf16[272,256]{1,0:T(8,128)(2,1)S(1)}, u32[]{:S(2)}, u32[]{:S(2)}) %collective-permute-start.6) | collective-permute-done | bytes 139296 | tf_op jit(solution)/shard_map/ppermute | solution.py:245
  27.4 0.0 collective-permute-done.7.other_ref
  27.4 0.6 %attend.1 = bf16[8,32,256]{2,1,0:T(8,128)(2,1)S(1)} custom-call(bf16[272,256]{1,0:T(8,128)(2,1)S(1)} %add_convert_fusion.own_ref, bf16[272,256]{1,0:T(8,128)(2,1)S(1)} %collective-permute-done.6.got_ref, bf16[128,128]{1,0:T(8,128)(2,1)S(1)} %bitcast.13, bf16[128,128]{1,0:T(8,128)(2,1)S(1)} %collective-permute-done.7.other_ref, ...), custom_call_target="tpu_custom_call" | custom-call | tf_op jit(solution)/shard_map/attend/pallas_call | solution.py:195
  28.0 8.3 %all_to_all.5.got_ref = bf16[8,32,256]{2,1,0:T(8,128)(2,1)S(1)} all-to-all(bf16[8,32,256]{2,1,0:T(8,128)(2,1)S(1)} %attend.1), channel_id=1, replica_groups={{0,1,2,3,4,5,6,7},{8,9,10,11,12,13,14,15},{16,17,18,19,20,21,22,23},{24..., dimensions={0} | all-to-all | bytes 262144 | tf_op jit(solution)/shard_map/all_to_all | solution.py:279
  36.3 1.0 %rank.1 = f32[2,32]{1,0:T(2,128)} custom-call(bf16[8,32,256]{2,1,0:T(8,128)(2,1)S(1)} %all_to_all.5.got_ref, f32[64,512]{1,0:T(8,128)S(1)} %convolution_add_fusion.base_ref, bf16[256,512]{1,0:T(8,128)(2,1)S(1)} %copy-done, f32[1,512]{1,0:T(1,128)S(1)} %bitcast.14), custom_call_target="tpu_custom_call" | custom-call | tf_op jit(solution)/shard_map/rank/pallas_call | solution.py:231
  (9 shorter events, 0.1 us)
Async XLA Ops:
  0.7 10.9 %copy-start.4 = (bf16[2,32,128]{2,1,0:T(8,128)(2,1)S(1)}, bf16[2,32,128]{2,1,0:T(8,128)(2,1)}, u32[]{:S(2)}) copy-start(bf16[2,32,128]{2,1,0:T(8,128)(2,1)} %param.12) | copy-start | bytes 49156
  4.2 18.8 %copy-start = (bf16[256,512]{1,0:T(8,128)(2,1)S(1)}, bf16[256,512]{1,0:T(8,128)(2,1)}, u32[]{:S(2)}) copy-start(bf16[256,512]{1,0:T(8,128)(2,1)} %wh_ref.1) | copy-start | bytes 786436
  4.2 18.8 %copy-start.5 = (f32[512]{0:T(512)S(1)}, f32[512]{0:T(512)}, u32[]{:S(2)}) copy-start(f32[512]{0:T(512)} %param.16) | copy-start | bytes 6148
  4.2 23.2 %copy-start.1 = (bf16[128,128]{1,0:T(8,128)(2,1)S(1)}, bf16[128,128]{1,0:T(8,128)(2,1)}, u32[]{:S(2)}) copy-start(bf16[128,128]{1,0:T(8,128)(2,1)} %wq_ref.1) | copy-start | bytes 98308
  4.2 23.1 %copy-start.2 = (bf16[128,128]{1,0:T(8,128)(2,1)S(1)}, bf16[128,128]{1,0:T(8,128)(2,1)}, u32[]{:S(2)}) copy-start(bf16[128,128]{1,0:T(8,128)(2,1)} %wk_ref.1) | copy-start | bytes 98308
  4.2 32.1 %copy-start.3 = (f32[512]{0:T(512)S(1)}, f32[512]{0:T(512)}, u32[]{:S(2)}) copy-start(f32[512]{0:T(512)} %param.17) | copy-start | bytes 6148
  4.2 1.9 %collective-permute-start = (bf16[272,256]{1,0:T(8,128)(2,1)S(1)}, bf16[272,256]{1,0:T(8,128)(2,1)S(1)}, u32[]{:S(2)}, u32[]{:S(2)}) collective-permute-start(bf16[272,256]{1,0:T(8,128)(2,1)S(1)} %get-tuple-element.23), channel_id=1, source_target_pairs={{0,2},{2,0},{4,6},{6,4},{8,10},{10,8},{12,14},{14,12},{16,18},{18,... | collective-permute-start | bytes 417800 | tf_op jit(solution)/shard_map/ppermute | solution.py:245
  6.2 6.9 %collective-permute-start.3 = (bf16[272,256]{1,0:T(8,128)(2,1)S(1)}, bf16[272,256]{1,0:T(8,128)(2,1)S(1)}, u32[]{:S(2)}, u32[]{:S(2)}) collective-permute-start(bf16[272,256]{1,0:T(8,128)(2,1)S(1)} %add_convert_fusion.2), channel_id=1, source_target_pairs={{0,4},{2,6},{4,0},{6,2},{8,12},{10,14},{12,8},{14,10},{16,20},{18,... | collective-permute-start | bytes 417800 | tf_op jit(solution)/shard_map/ppermute | solution.py:245
  11.2 1.9 %collective-permute-start.2 = (bf16[272,256]{1,0:T(8,128)(2,1)S(1)}, bf16[272,256]{1,0:T(8,128)(2,1)S(1)}, u32[]{:S(2)}, u32[]{:S(2)}) collective-permute-start(bf16[272,256]{1,0:T(8,128)(2,1)S(1)} %get-tuple-element.28), channel_id=1, source_target_pairs={{0,2},{2,0},{4,6},{6,4},{8,10},{10,8},{12,14},{14,12},{16,18},{18,... | collective-permute-start | bytes 417800 | tf_op jit(solution)/shard_map/ppermute | solution.py:245
  11.5 1.2 %collective-permute-start.1 = (bf16[2,32,128]{2,1,0:T(8,128)(2,1)S(1)}, bf16[2,32,128]{2,1,0:T(8,128)(2,1)S(1)}, u32[]{:S(2)}, u32[]{:S(2)}) collective-permute-start(bf16[2,32,128]{2,1,0:T(8,128)(2,1)S(1)} %copy-done.4), channel_id=1, source_target_pairs={{0,2},{2,0},{4,6},{6,4},{8,10},{10,8},{12,14},{14,12},{16,18},{18,... | collective-permute-start | bytes 49160 | tf_op jit(solution)/shard_map/ppermute | solution.py:245
  13.2 5.6 %collective-permute-start.5 = (bf16[272,256]{1,0:T(8,128)(2,1)S(1)}, bf16[272,256]{1,0:T(8,128)(2,1)S(1)}, u32[]{:S(2)}, u32[]{:S(2)}) collective-permute-start(bf16[272,256]{1,0:T(8,128)(2,1)S(1)} %add_convert_fusion.1), channel_id=1, source_target_pairs={{0,8},{2,10},{4,12},{6,14},{8,0},{10,2},{12,4},{14,6},{16,24},{18,... | collective-permute-start | bytes 417800 | tf_op jit(solution)/shard_map/ppermute | solution.py:245
  15.1 3.7 %collective-permute-start.4 = (bf16[2,32,128]{2,1,0:T(8,128)(2,1)S(1)}, bf16[2,32,128]{2,1,0:T(8,128)(2,1)S(1)}, u32[]{:S(2)}, u32[]{:S(2)}) collective-permute-start(bf16[2,32,128]{2,1,0:T(8,128)(2,1)S(1)} %get-tuple-element.38), channel_id=1, source_target_pairs={{0,1},{1,0},{2,3},{3,2},{4,5},{5,4},{6,7},{7,6},{8,9},{9,8},{10,11... | collective-permute-start | bytes 49160 | tf_op jit(solution)/shard_map/ppermute | solution.py:245
  18.8 8.5 %collective-permute-start.6 = (bf16[272,256]{1,0:T(8,128)(2,1)S(1)}, bf16[272,256]{1,0:T(8,128)(2,1)S(1)}, u32[]{:S(2)}, u32[]{:S(2)}) collective-permute-start(bf16[272,256]{1,0:T(8,128)(2,1)S(1)} %add_convert_fusion.own_ref), channel_id=1, source_target_pairs={{0,16},{2,18},{4,20},{6,22},{8,24},{10,26},{12,28},{14,30},{16,0},... | collective-permute-start | bytes 417800 | tf_op jit(solution)/shard_map/ppermute | solution.py:245
  21.5 5.9 %collective-permute-start.7 = (bf16[128,128]{1,0:T(8,128)(2,1)S(1)}, bf16[128,128]{1,0:T(8,128)(2,1)S(1)}, u32[]{:S(2)}, u32[]{:S(2)}) collective-permute-start(bf16[128,128]{1,0:T(8,128)(2,1)S(1)} %bitcast.12), channel_id=1, source_target_pairs={{0,4},{2,6},{4,0},{6,2},{8,12},{10,14},{12,8},{14,10},{16,20},{18,... | collective-permute-start | bytes 98312 | tf_op jit(solution)/shard_map/ppermute | solution.py:245

commit v5 on v4

--- a/solution.py
+++ b/solution.py
@@ -67,10 +67,11 @@
     step, steps = pl.program_id(0), pl.num_programs(0)
     block, width = rows_ref.shape
     turned = jnp.transpose(rows_ref[...].astype(BF))
-    turned_ref[...] = turned
+    there = pl.ds(pl.multiple_of(step * block, block), block)
+    turned_ref[:, there] = turned
     slot = step * block + lax.broadcasted_iota(jnp.int32, ids_ref.shape, 1)
     marked = jnp.where(slot < live_ref[0, 0], ids_ref[...] ^ (flip_of("seq") * low), -1)
-    marked_ref[...] = marked
+    marked_ref[:, there] = marked
     high, within = split(marked, 2 * SHARERS - 2, low)
     part = pooled(turned, high, within, low, 2)
 
@@ -118,9 +119,9 @@
             pl.BlockSpec((block, width), lambda b: (b, 0)),
         ],
         out_specs=[
-            pl.BlockSpec((height, low), lambda b: (0, 0)),
-            pl.BlockSpec((width, block), lambda b: (0, b)),
-            pl.BlockSpec((1, block), lambda b: (0, b)),
+            pl.BlockSpec(memory_space=pltpu.VMEM),
+            pl.BlockSpec(memory_space=pltpu.VMEM),
+            pl.BlockSpec(memory_space=pltpu.VMEM),
         ],
         out_shape=[
             jax.ShapeDtypeStruct((height, low), BF),

time: 37.4 us -> 37.3 us (level)
  no operation moved by 1% of the time
where the time goes in v5:
time: 37.3 us; the launch traced here: 37.2 us
  starting transfers between devices  11.2 us (30%)
  Pallas kernels  8.85 us (24%)
  blocking collectives  8.28 us (22%)
  waiting for transfers between devices  7.73 us (21%)
  between operations  0.77 us (2%)
    ppermute x8, starting transfers between devices, swap(): return lax.ppermute(value, axis, [(i, i ^ step) for i in range(count)])  11.2 us
    all_to_all x1, blocking collectives, on_device(): lax.all_to_all(partial, ('seq', 'cand'), 0, 0, tiled=True, axis_index_gro...  8.28 us
    ppermute x8, waiting for transfers between devices, swap(): return lax.ppermute(value, axis, [(i, i ^ step) for i in range(count)])  7.73 us
    pallas_call x2, Pallas kernels, pool_next(): pl.pallas_call(functools.partial(next_kernel, low, *plan, min(NEXT_BLOCK,...  3.83 us
    pallas_call x1, Pallas kernels, pool_first(): pl.pallas_call(functools.partial(first_kernel, low, *plan), grid=(slots /...  3.39 us
    pallas_call x1, Pallas kernels, rank(): pl.pallas_call(functools.partial(rank_kernel, users), out_shape=jax.Shape...  0.98 us
  transfers between devices with their start and end apart: 8, of which 4 were waited for; matrix products, arithmetic and copies ran while one was open for 0% of the time, Pallas kernels for 10%

profile of v5, /device:TPU:0, one launch (start us, length us, event | category | flops | bytes accessed | tf_op | source)
XLA Modules:
  0.0 37.2 jit_solution(18154786121267140862)
XLA Ops:
  0.7 0.0 copy-start.4
  0.7 3.4 %pool_first.1 = (bf16[272,256]{1,0:T(8,128)(2,1)S(1)}, bf16[128,8192]{1,0:T(8,128)(2,1)S(1)}, s32[1,8192]{1,0:T(1,128)S(1)}) custom-call(s32[1,1]{1,0:T(1,128)S(6)} %copy.10.live_ref, s32[1,8192]{1,0:T(1,128)} %ids_ref.1, f32[8192,128]{1,0:T(8,128)} %bitcast.15), custom_call_target="tpu_custom_call" | custom-call | tf_op jit(solution)/shard_map/pool_first/pallas_call | solution.py:113
  4.1 0.0 copy-start
  4.1 0.0 copy-start.5
  4.1 0.0 copy-start.1
  4.1 0.0 copy-start.2
  4.1 0.0 copy-start.3
  4.1 0.5 %collective-permute-start = (bf16[272,256]{1,0:T(8,128)(2,1)S(1)}, bf16[272,256]{1,0:T(8,128)(2,1)S(1)}, u32[]{:S(2)}, u32[]{:S(2)}) collective-permute-start(bf16[272,256]{1,0:T(8,128)(2,1)S(1)} %get-tuple-element.23), channel_id=1, source_target_pairs={{0,2},{2,0},{4,6},{6,4},{8,10},{10,8},{12,14},{14,12},{16,18},{18,... | collective-permute-start | bytes 417800 | tf_op jit(solution)/shard_map/ppermute | solution.py:246
  4.6 1.4 %pool_next.3 = f32[272,256]{1,0:T(8,128)S(1)} custom-call(s32[1,8192]{1,0:T(1,128)S(1)} %get-tuple-element.21.marked_ref, bf16[128,8192]{1,0:T(8,128)(2,1)S(1)} %get-tuple-element.24.turned_ref), custom_call_target="tpu_custom_call" | custom-call | tf_op jit(solution)/shard_map/pool_next/pallas_call | solution.py:142
  6.0 0.0 collective-permute-done
  6.0 2.6 %collective-permute-start.3 = (bf16[272,256]{1,0:T(8,128)(2,1)S(1)}, bf16[272,256]{1,0:T(8,128)(2,1)S(1)}, u32[]{:S(2)}, u32[]{:S(2)}) collective-permute-start(bf16[272,256]{1,0:T(8,128)(2,1)S(1)} %add_convert_fusion.2), channel_id=1, source_target_pairs={{0,4},{2,6},{4,0},{6,2},{8,12},{10,14},{12,8},{14,10},{16,20},{18,... | collective-permute-start | bytes 417800 | tf_op jit(solution)/shard_map/ppermute | solution.py:246
  8.6 2.5 %pool_next.2 = (f32[272,256]{1,0:T(8,128)S(1)}, bf16[272,256]{1,0:T(8,128)(2,1)S(1)}) custom-call(s32[1,8192]{1,0:T(1,128)S(1)} %get-tuple-element.21.marked_ref, bf16[128,8192]{1,0:T(8,128)(2,1)S(1)} %get-tuple-element.24.turned_ref), custom_call_target="tpu_custom_call" | custom-call | tf_op jit(solution)/shard_map/pool_next/pallas_call | solution.py:142
  11.1 0.3 collective-permute-start.2
  11.4 0.3 collective-permute-start.1
  11.7 0.9 %collective-permute-done.1 = bf16[2,32,128]{2,1,0:T(8,128)(2,1)S(1)} collective-permute-done((bf16[2,32,128]{2,1,0:T(8,128)(2,1)S(1)}, bf16[2,32,128]{2,1,0:T(8,128)(2,1)S(1)}, u32[]{:S(2)}, u32[]{:S(2)}) %collective-permute-start.1) | collective-permute-done | bytes 16416 | tf_op jit(solution)/shard_map/ppermute | solution.py:246
  12.6 0.4 %collective-permute-done.3 = bf16[272,256]{1,0:T(8,128)(2,1)S(1)} collective-permute-done((bf16[272,256]{1,0:T(8,128)(2,1)S(1)}, bf16[272,256]{1,0:T(8,128)(2,1)S(1)}, u32[]{:S(2)}, u32[]{:S(2)}) %collective-permute-start.3) | collective-permute-done | bytes 139296 | tf_op jit(solution)/shard_map/ppermute | solution.py:246
  13.0 0.0 collective-permute-done.2
  13.0 0.1 add_convert_fusion.1
  13.0 1.9 %collective-permute-start.5 = (bf16[272,256]{1,0:T(8,128)(2,1)S(1)}, bf16[272,256]{1,0:T(8,128)(2,1)S(1)}, u32[]{:S(2)}, u32[]{:S(2)}) collective-permute-start(bf16[272,256]{1,0:T(8,128)(2,1)S(1)} %add_convert_fusion.1), channel_id=1, source_target_pairs={{0,8},{2,10},{4,12},{6,14},{8,0},{10,2},{12,4},{14,6},{16,24},{18,... | collective-permute-start | bytes 417800 | tf_op jit(solution)/shard_map/ppermute | solution.py:246
  14.9 1.5 %collective-permute-start.4 = (bf16[2,32,128]{2,1,0:T(8,128)(2,1)S(1)}, bf16[2,32,128]{2,1,0:T(8,128)(2,1)S(1)}, u32[]{:S(2)}, u32[]{:S(2)}) collective-permute-start(bf16[2,32,128]{2,1,0:T(8,128)(2,1)S(1)} %get-tuple-element.38), channel_id=1, source_target_pairs={{0,1},{1,0},{2,3},{3,2},{4,5},{5,4},{6,7},{7,6},{8,9},{9,8},{10,11... | collective-permute-start | bytes 49160 | tf_op jit(solution)/shard_map/ppermute | solution.py:246
  16.4 2.2 %collective-permute-done.4 = bf16[2,32,128]{2,1,0:T(8,128)(2,1)S(1)} collective-permute-done((bf16[2,32,128]{2,1,0:T(8,128)(2,1)S(1)}, bf16[2,32,128]{2,1,0:T(8,128)(2,1)S(1)}, u32[]{:S(2)}, u32[]{:S(2)}) %collective-permute-start.4) | collective-permute-done | bytes 16416 | tf_op jit(solution)/shard_map/ppermute | solution.py:246
  18.7 0.0 collective-permute-done.5
  18.7 2.7 %collective-permute-start.6 = (bf16[272,256]{1,0:T(8,128)(2,1)S(1)}, bf16[272,256]{1,0:T(8,128)(2,1)S(1)}, u32[]{:S(2)}, u32[]{:S(2)}) collective-permute-start(bf16[272,256]{1,0:T(8,128)(2,1)S(1)} %add_convert_fusion.own_ref), channel_id=1, source_target_pairs={{0,16},{2,18},{4,20},{6,22},{8,24},{10,26},{12,28},{14,30},{16,0},... | collective-permute-start | bytes 417800 | tf_op jit(solution)/shard_map/ppermute | solution.py:246
  21.4 1.5 %collective-permute-start.7 = (bf16[128,128]{1,0:T(8,128)(2,1)S(1)}, bf16[128,128]{1,0:T(8,128)(2,1)S(1)}, u32[]{:S(2)}, u32[]{:S(2)}) collective-permute-start(bf16[128,128]{1,0:T(8,128)(2,1)S(1)} %bitcast.12), channel_id=1, source_target_pairs={{0,4},{2,6},{4,0},{6,2},{8,12},{10,14},{12,8},{14,10},{16,20},{18,... | collective-permute-start | bytes 98312 | tf_op jit(solution)/shard_map/ppermute | solution.py:246
  22.9 0.0 copy-done.5
  22.9 0.1 convolution_add_fusion.base_ref
  23.0 4.2 %collective-permute-done.6.got_ref = bf16[272,256]{1,0:T(8,128)(2,1)S(1)} collective-permute-done((bf16[272,256]{1,0:T(8,128)(2,1)S(1)}, bf16[272,256]{1,0:T(8,128)(2,1)S(1)}, u32[]{:S(2)}, u32[]{:S(2)}) %collective-permute-start.6) | collective-permute-done | bytes 139296 | tf_op jit(solution)/shard_map/ppermute | solution.py:246
  27.2 0.0 collective-permute-done.7.other_ref
  27.2 0.0 copy-done.1
  27.2 0.6 %attend.1 = bf16[8,32,256]{2,1,0:T(8,128)(2,1)S(1)} custom-call(bf16[272,256]{1,0:T(8,128)(2,1)S(1)} %add_convert_fusion.own_ref, bf16[272,256]{1,0:T(8,128)(2,1)S(1)} %collective-permute-done.6.got_ref, bf16[128,128]{1,0:T(8,128)(2,1)S(1)} %bitcast.13, bf16[128,128]{1,0:T(8,128)(2,1)S(1)} %collective-permute-done.7.other_ref, ...), custom_call_target="tpu_custom_call" | custom-call | tf_op jit(solution)/shard_map/attend/pallas_call | solution.py:196
  27.9 8.3 %all_to_all.5.got_ref = bf16[8,32,256]{2,1,0:T(8,128)(2,1)S(1)} all-to-all(bf16[8,32,256]{2,1,0:T(8,128)(2,1)S(1)} %attend.1), channel_id=1, replica_groups={{0,1,2,3,4,5,6,7},{8,9,10,11,12,13,14,15},{16,17,18,19,20,21,22,23},{24..., dimensions={0} | all-to-all | bytes 262144 | tf_op jit(solution)/shard_map/all_to_all | solution.py:280
  36.2 1.0 %rank.1 = f32[2,32]{1,0:T(2,128)} custom-call(bf16[8,32,256]{2,1,0:T(8,128)(2,1)S(1)} %all_to_all.5.got_ref, f32[64,512]{1,0:T(8,128)S(1)} %convolution_add_fusion.base_ref, bf16[256,512]{1,0:T(8,128)(2,1)S(1)} %copy-done, f32[1,512]{1,0:T(1,128)S(1)} %bitcast.14), custom_call_target="tpu_custom_call" | custom-call | tf_op jit(solution)/shard_map/rank/pallas_call | solution.py:232
  (9 shorter events, 0.1 us)
Async XLA Ops:
  0.7 10.7 %copy-start.4 = (bf16[2,32,128]{2,1,0:T(8,128)(2,1)S(1)}, bf16[2,32,128]{2,1,0:T(8,128)(2,1)}, u32[]{:S(2)}) copy-start(bf16[2,32,128]{2,1,0:T(8,128)(2,1)} %param.12) | copy-start | bytes 49156
  4.1 18.8 %copy-start = (bf16[256,512]{1,0:T(8,128)(2,1)S(1)}, bf16[256,512]{1,0:T(8,128)(2,1)}, u32[]{:S(2)}) copy-start(bf16[256,512]{1,0:T(8,128)(2,1)} %wh_ref.1) | copy-start | bytes 786436
  4.1 18.8 %copy-start.5 = (f32[512]{0:T(512)S(1)}, f32[512]{0:T(512)}, u32[]{:S(2)}) copy-start(f32[512]{0:T(512)} %param.16) | copy-start | bytes 6148
  4.1 23.2 %copy-start.1 = (bf16[128,128]{1,0:T(8,128)(2,1)S(1)}, bf16[128,128]{1,0:T(8,128)(2,1)}, u32[]{:S(2)}) copy-start(bf16[128,128]{1,0:T(8,128)(2,1)} %wq_ref.1) | copy-start | bytes 98308
  4.1 23.1 %copy-start.2 = (bf16[128,128]{1,0:T(8,128)(2,1)S(1)}, bf16[128,128]{1,0:T(8,128)(2,1)}, u32[]{:S(2)}) copy-start(bf16[128,128]{1,0:T(8,128)(2,1)} %wk_ref.1) | copy-start | bytes 98308
  4.1 32.1 %copy-start.3 = (f32[512]{0:T(512)S(1)}, f32[512]{0:T(512)}, u32[]{:S(2)}) copy-start(f32[512]{0:T(512)} %param.17) | copy-start | bytes 6148
  4.1 1.9 %collective-permute-start = (bf16[272,256]{1,0:T(8,128)(2,1)S(1)}, bf16[272,256]{1,0:T(8,128)(2,1)S(1)}, u32[]{:S(2)}, u32[]{:S(2)}) collective-permute-start(bf16[272,256]{1,0:T(8,128)(2,1)S(1)} %get-tuple-element.23), channel_id=1, source_target_pairs={{0,2},{2,0},{4,6},{6,4},{8,10},{10,8},{12,14},{14,12},{16,18},{18,... | collective-permute-start | bytes 417800 | tf_op jit(solution)/shard_map/ppermute | solution.py:246
  6.0 6.9 %collective-permute-start.3 = (bf16[272,256]{1,0:T(8,128)(2,1)S(1)}, bf16[272,256]{1,0:T(8,128)(2,1)S(1)}, u32[]{:S(2)}, u32[]{:S(2)}) collective-permute-start(bf16[272,256]{1,0:T(8,128)(2,1)S(1)} %add_convert_fusion.2), channel_id=1, source_target_pairs={{0,4},{2,6},{4,0},{6,2},{8,12},{10,14},{12,8},{14,10},{16,20},{18,... | collective-permute-start | bytes 417800 | tf_op jit(solution)/shard_map/ppermute | solution.py:246
  11.1 1.9 %collective-permute-start.2 = (bf16[272,256]{1,0:T(8,128)(2,1)S(1)}, bf16[272,256]{1,0:T(8,128)(2,1)S(1)}, u32[]{:S(2)}, u32[]{:S(2)}) collective-permute-start(bf16[272,256]{1,0:T(8,128)(2,1)S(1)} %get-tuple-element.28), channel_id=1, source_target_pairs={{0,2},{2,0},{4,6},{6,4},{8,10},{10,8},{12,14},{14,12},{16,18},{18,... | collective-permute-start | bytes 417800 | tf_op jit(solution)/shard_map/ppermute | solution.py:246
  11.4 1.2 %collective-permute-start.1 = (bf16[2,32,128]{2,1,0:T(8,128)(2,1)S(1)}, bf16[2,32,128]{2,1,0:T(8,128)(2,1)S(1)}, u32[]{:S(2)}, u32[]{:S(2)}) collective-permute-start(bf16[2,32,128]{2,1,0:T(8,128)(2,1)S(1)} %copy-done.4), channel_id=1, source_target_pairs={{0,2},{2,0},{4,6},{6,4},{8,10},{10,8},{12,14},{14,12},{16,18},{18,... | collective-permute-start | bytes 49160 | tf_op jit(solution)/shard_map/ppermute | solution.py:246
  13.0 5.6 %collective-permute-start.5 = (bf16[272,256]{1,0:T(8,128)(2,1)S(1)}, bf16[272,256]{1,0:T(8,128)(2,1)S(1)}, u32[]{:S(2)}, u32[]{:S(2)}) collective-permute-start(bf16[272,256]{1,0:T(8,128)(2,1)S(1)} %add_convert_fusion.1), channel_id=1, source_target_pairs={{0,8},{2,10},{4,12},{6,14},{8,0},{10,2},{12,4},{14,6},{16,24},{18,... | collective-permute-start | bytes 417800 | tf_op jit(solution)/shard_map/ppermute | solution.py:246
  14.9 3.7 %collective-permute-start.4 = (bf16[2,32,128]{2,1,0:T(8,128)(2,1)S(1)}, bf16[2,32,128]{2,1,0:T(8,128)(2,1)S(1)}, u32[]{:S(2)}, u32[]{:S(2)}) collective-permute-start(bf16[2,32,128]{2,1,0:T(8,128)(2,1)S(1)} %get-tuple-element.38), channel_id=1, source_target_pairs={{0,1},{1,0},{2,3},{3,2},{4,5},{5,4},{6,7},{7,6},{8,9},{9,8},{10,11... | collective-permute-start | bytes 49160 | tf_op jit(solution)/shard_map/ppermute | solution.py:246
  18.7 8.5 %collective-permute-start.6 = (bf16[272,256]{1,0:T(8,128)(2,1)S(1)}, bf16[272,256]{1,0:T(8,128)(2,1)S(1)}, u32[]{:S(2)}, u32[]{:S(2)}) collective-permute-start(bf16[272,256]{1,0:T(8,128)(2,1)S(1)} %add_convert_fusion.own_ref), channel_id=1, source_target_pairs={{0,16},{2,18},{4,20},{6,22},{8,24},{10,26},{12,28},{14,30},{16,0},... | collective-permute-start | bytes 417800 | tf_op jit(solution)/shard_map/ppermute | solution.py:246
  21.4 5.9 %collective-permute-start.7 = (bf16[128,128]{1,0:T(8,128)(2,1)S(1)}, bf16[128,128]{1,0:T(8,128)(2,1)S(1)}, u32[]{:S(2)}, u32[]{:S(2)}) collective-permute-start(bf16[128,128]{1,0:T(8,128)(2,1)S(1)} %bitcast.12), channel_id=1, source_target_pairs={{0,4},{2,6},{4,0},{6,2},{8,12},{10,14},{12,8},{14,10},{16,20},{18,... | collective-permute-start | bytes 98312 | tf_op jit(solution)/shard_map/ppermute | solution.py:246

commit v6 on v5

--- a/solution.py
+++ b/solution.py
@@ -257,7 +257,8 @@
     candidates_in, send = after(candidates, send)
     got = swap(send, 1)
     asked = jnp.stack([candidates_in, swap(candidates_in, 1)], 1)
-    own = (mine + got.astype(F32) + beside.astype(F32)).astype(BF)
+    used = 2 * behaviors.shape[2] + 2 * digits
+    own = (mine[:used] + got[:used].astype(F32) + beside[:used].astype(F32)).astype(BF)
     asked, own = after(asked, own)
     step = SHARERS
     got = swap(own, step)

time: 37.3 us -> 37.1 us (level)
  no operation moved by 1% of the time
where the time goes in v6:
time: 37.1 us; the launch traced here: 36.9 us
  starting transfers between devices  11.2 us (30%)
  Pallas kernels  8.86 us (24%)
  blocking collectives  8.28 us (22%)
  waiting for transfers between devices  7.47 us (20%)
  between operations  0.77 us (2%)
    ppermute x8, starting transfers between devices, swap(): return lax.ppermute(value, axis, [(i, i ^ step) for i in range(count)])  11.2 us
    all_to_all x1, blocking collectives, on_device(): lax.all_to_all(partial, ('seq', 'cand'), 0, 0, tiled=True, axis_index_gro...  8.28 us
    ppermute x8, waiting for transfers between devices, swap(): return lax.ppermute(value, axis, [(i, i ^ step) for i in range(count)])  7.47 us
    pallas_call x2, Pallas kernels, pool_next(): pl.pallas_call(functools.partial(next_kernel, low, *plan, min(NEXT_BLOCK,...  3.83 us
    pallas_call x1, Pallas kernels, pool_first(): pl.pallas_call(functools.partial(first_kernel, low, *plan), grid=(slots /...  3.39 us
    pallas_call x1, Pallas kernels, rank(): pl.pallas_call(functools.partial(rank_kernel, users), out_shape=jax.Shape...  0.98 us
  transfers between devices with their start and end apart: 8, of which 4 were waited for; matrix products, arithmetic and copies ran while one was open for 0% of the time, Pallas kernels for 10%

profile of v6, /device:TPU:0, one launch (start us, length us, event | category | flops | bytes accessed | tf_op | source)
XLA Modules:
  0.0 36.9 jit_solution(10999420864372195898)
XLA Ops:
  0.7 0.0 copy-start.4
  0.7 3.4 %pool_first.1 = (bf16[272,256]{1,0:T(8,128)(2,1)S(1)}, bf16[128,8192]{1,0:T(8,128)(2,1)S(1)}, s32[1,8192]{1,0:T(1,128)S(1)}) custom-call(s32[1,1]{1,0:T(1,128)S(6)} %copy.10.live_ref, s32[1,8192]{1,0:T(1,128)} %ids_ref.1, f32[8192,128]{1,0:T(8,128)} %bitcast.15), custom_call_target="tpu_custom_call" | custom-call | tf_op jit(solution)/shard_map/pool_first/pallas_call | solution.py:113
  4.1 0.0 copy-start
  4.1 0.0 copy-start.5
  4.1 0.0 copy-start.1
  4.1 0.0 copy-start.2
  4.1 0.0 copy-start.3
  4.1 0.5 %collective-permute-start = (bf16[272,256]{1,0:T(8,128)(2,1)S(1)}, bf16[272,256]{1,0:T(8,128)(2,1)S(1)}, u32[]{:S(2)}, u32[]{:S(2)}) collective-permute-start(bf16[272,256]{1,0:T(8,128)(2,1)S(1)} %get-tuple-element.23), channel_id=1, source_target_pairs={{0,2},{2,0},{4,6},{6,4},{8,10},{10,8},{12,14},{14,12},{16,18},{18,... | collective-permute-start | bytes 417800 | tf_op jit(solution)/shard_map/ppermute | solution.py:246
  4.6 1.4 %pool_next.3 = f32[272,256]{1,0:T(8,128)S(1)} custom-call(s32[1,8192]{1,0:T(1,128)S(1)} %get-tuple-element.21.marked_ref, bf16[128,8192]{1,0:T(8,128)(2,1)S(1)} %get-tuple-element.24.turned_ref), custom_call_target="tpu_custom_call" | custom-call | tf_op jit(solution)/shard_map/pool_next/pallas_call | solution.py:142
  6.0 0.0 collective-permute-done
  6.0 2.6 %collective-permute-start.3 = (bf16[272,256]{1,0:T(8,128)(2,1)S(1)}, bf16[272,256]{1,0:T(8,128)(2,1)S(1)}, u32[]{:S(2)}, u32[]{:S(2)}) collective-permute-start(bf16[272,256]{1,0:T(8,128)(2,1)S(1)} %add_convert_fusion), channel_id=1, source_target_pairs={{0,4},{2,6},{4,0},{6,2},{8,12},{10,14},{12,8},{14,10},{16,20},{18,... | collective-permute-start | bytes 417800 | tf_op jit(solution)/shard_map/ppermute | solution.py:246
  8.6 2.5 %pool_next.2 = (f32[272,256]{1,0:T(8,128)S(1)}, bf16[272,256]{1,0:T(8,128)(2,1)S(1)}) custom-call(s32[1,8192]{1,0:T(1,128)S(1)} %get-tuple-element.21.marked_ref, bf16[128,8192]{1,0:T(8,128)(2,1)S(1)} %get-tuple-element.24.turned_ref), custom_call_target="tpu_custom_call" | custom-call | tf_op jit(solution)/shard_map/pool_next/pallas_call | solution.py:142
  11.1 0.3 collective-permute-start.2
  11.4 0.0 copy-done.4
  11.4 0.3 collective-permute-start.1
  11.7 0.9 %collective-permute-done.1 = bf16[2,32,128]{2,1,0:T(8,128)(2,1)S(1)} collective-permute-done((bf16[2,32,128]{2,1,0:T(8,128)(2,1)S(1)}, bf16[2,32,128]{2,1,0:T(8,128)(2,1)S(1)}, u32[]{:S(2)}, u32[]{:S(2)}) %collective-permute-start.1) | collective-permute-done | bytes 16416 | tf_op jit(solution)/shard_map/ppermute | solution.py:246
  12.6 0.4 %collective-permute-done.3 = bf16[272,256]{1,0:T(8,128)(2,1)S(1)} collective-permute-done((bf16[272,256]{1,0:T(8,128)(2,1)S(1)}, bf16[272,256]{1,0:T(8,128)(2,1)S(1)}, u32[]{:S(2)}, u32[]{:S(2)}) %collective-permute-start.3) | collective-permute-done | bytes 139296 | tf_op jit(solution)/shard_map/ppermute | solution.py:246
  13.0 0.0 collective-permute-done.2
  13.0 0.1 add_convert_fusion.2
  13.0 1.9 %collective-permute-start.5 = (bf16[264,256]{1,0:T(8,128)(2,1)S(1)}, bf16[264,256]{1,0:T(8,128)(2,1)S(1)}, u32[]{:S(2)}, u32[]{:S(2)}) collective-permute-start(bf16[264,256]{1,0:T(8,128)(2,1)S(1)} %add_convert_fusion.2), channel_id=1, source_target_pairs={{0,8},{2,10},{4,12},{6,14},{8,0},{10,2},{12,4},{14,6},{16,24},{18,... | collective-permute-start | bytes 405512 | tf_op jit(solution)/shard_map/ppermute | solution.py:246
  14.9 1.5 %collective-permute-start.4 = (bf16[2,32,128]{2,1,0:T(8,128)(2,1)S(1)}, bf16[2,32,128]{2,1,0:T(8,128)(2,1)S(1)}, u32[]{:S(2)}, u32[]{:S(2)}) collective-permute-start(bf16[2,32,128]{2,1,0:T(8,128)(2,1)S(1)} %get-tuple-element.38), channel_id=1, source_target_pairs={{0,1},{1,0},{2,3},{3,2},{4,5},{5,4},{6,7},{7,6},{8,9},{9,8},{10,11... | collective-permute-start | bytes 49160 | tf_op jit(solution)/shard_map/ppermute | solution.py:246
  16.4 2.2 %collective-permute-done.4 = bf16[2,32,128]{2,1,0:T(8,128)(2,1)S(1)} collective-permute-done((bf16[2,32,128]{2,1,0:T(8,128)(2,1)S(1)}, bf16[2,32,128]{2,1,0:T(8,128)(2,1)S(1)}, u32[]{:S(2)}, u32[]{:S(2)}) %collective-permute-start.4) | collective-permute-done | bytes 16416 | tf_op jit(solution)/shard_map/ppermute | solution.py:246
  18.7 0.0 collective-permute-done.5
  18.7 2.7 %collective-permute-start.6 = (bf16[264,256]{1,0:T(8,128)(2,1)S(1)}, bf16[264,256]{1,0:T(8,128)(2,1)S(1)}, u32[]{:S(2)}, u32[]{:S(2)}) collective-permute-start(bf16[264,256]{1,0:T(8,128)(2,1)S(1)} %add_convert_fusion.1.own_ref), channel_id=1, source_target_pairs={{0,16},{2,18},{4,20},{6,22},{8,24},{10,26},{12,28},{14,30},{16,0},... | collective-permute-start | bytes 405512 | tf_op jit(solution)/shard_map/ppermute | solution.py:246
  21.4 1.5 %collective-permute-start.7 = (bf16[128,128]{1,0:T(8,128)(2,1)S(1)}, bf16[128,128]{1,0:T(8,128)(2,1)S(1)}, u32[]{:S(2)}, u32[]{:S(2)}) collective-permute-start(bf16[128,128]{1,0:T(8,128)(2,1)S(1)} %bitcast.12), channel_id=1, source_target_pairs={{0,4},{2,6},{4,0},{6,2},{8,12},{10,14},{12,8},{14,10},{16,20},{18,... | collective-permute-start | bytes 98312 | tf_op jit(solution)/shard_map/ppermute | solution.py:246
  22.8 0.0 copy-done
  22.9 0.1 convolution_add_fusion.base_ref
  23.0 4.0 %collective-permute-done.6.got_ref = bf16[264,256]{1,0:T(8,128)(2,1)S(1)} collective-permute-done((bf16[264,256]{1,0:T(8,128)(2,1)S(1)}, bf16[264,256]{1,0:T(8,128)(2,1)S(1)}, u32[]{:S(2)}, u32[]{:S(2)}) %collective-permute-start.6) | collective-permute-done | bytes 135200 | tf_op jit(solution)/shard_map/ppermute | solution.py:246
  27.0 0.0 collective-permute-done.7.other_ref
  27.0 0.7 %attend.1 = bf16[8,32,256]{2,1,0:T(8,128)(2,1)S(1)} custom-call(bf16[264,256]{1,0:T(8,128)(2,1)S(1)} %add_convert_fusion.1.own_ref, bf16[264,256]{1,0:T(8,128)(2,1)S(1)} %collective-permute-done.6.got_ref, bf16[128,128]{1,0:T(8,128)(2,1)S(1)} %bitcast.13, bf16[128,128]{1,0:T(8,128)(2,1)S(1)} %collective-permute-done.7.other_ref, ...), custom_call_target="tpu_custom_call" | custom-call | tf_op jit(solution)/shard_map/attend/pallas_call | solution.py:196
  27.6 8.3 %all_to_all.5.got_ref = bf16[8,32,256]{2,1,0:T(8,128)(2,1)S(1)} all-to-all(bf16[8,32,256]{2,1,0:T(8,128)(2,1)S(1)} %attend.1), channel_id=1, replica_groups={{0,1,2,3,4,5,6,7},{8,9,10,11,12,13,14,15},{16,17,18,19,20,21,22,23},{24..., dimensions={0} | all-to-all | bytes 262144 | tf_op jit(solution)/shard_map/all_to_all | solution.py:281
  35.9 1.0 %rank.1 = f32[2,32]{1,0:T(2,128)} custom-call(bf16[8,32,256]{2,1,0:T(8,128)(2,1)S(1)} %all_to_all.5.got_ref, f32[64,512]{1,0:T(8,128)S(1)} %convolution_add_fusion.base_ref, bf16[256,512]{1,0:T(8,128)(2,1)S(1)} %copy-done, f32[1,512]{1,0:T(1,128)S(1)} %bitcast.14), custom_call_target="tpu_custom_call" | custom-call | tf_op jit(solution)/shard_map/rank/pallas_call | solution.py:232
  (9 shorter events, 0.1 us)
Async XLA Ops:
  0.7 10.7 %copy-start.4 = (bf16[2,32,128]{2,1,0:T(8,128)(2,1)S(1)}, bf16[2,32,128]{2,1,0:T(8,128)(2,1)}, u32[]{:S(2)}) copy-start(bf16[2,32,128]{2,1,0:T(8,128)(2,1)} %param.12) | copy-start | bytes 49156
  4.1 18.8 %copy-start = (bf16[256,512]{1,0:T(8,128)(2,1)S(1)}, bf16[256,512]{1,0:T(8,128)(2,1)}, u32[]{:S(2)}) copy-start(bf16[256,512]{1,0:T(8,128)(2,1)} %wh_ref.1) | copy-start | bytes 786436
  4.1 18.8 %copy-start.5 = (f32[512]{0:T(512)S(1)}, f32[512]{0:T(512)}, u32[]{:S(2)}) copy-start(f32[512]{0:T(512)} %param.16) | copy-start | bytes 6148
  4.1 22.9 %copy-start.1 = (bf16[128,128]{1,0:T(8,128)(2,1)S(1)}, bf16[128,128]{1,0:T(8,128)(2,1)}, u32[]{:S(2)}) copy-start(bf16[128,128]{1,0:T(8,128)(2,1)} %wq_ref.1) | copy-start | bytes 98308
  4.1 22.9 %copy-start.2 = (bf16[128,128]{1,0:T(8,128)(2,1)S(1)}, bf16[128,128]{1,0:T(8,128)(2,1)}, u32[]{:S(2)}) copy-start(bf16[128,128]{1,0:T(8,128)(2,1)} %wk_ref.1) | copy-start | bytes 98308
  4.1 31.8 %copy-start.3 = (f32[512]{0:T(512)S(1)}, f32[512]{0:T(512)}, u32[]{:S(2)}) copy-start(f32[512]{0:T(512)} %param.17) | copy-start | bytes 6148
  4.1 1.9 %collective-permute-start = (bf16[272,256]{1,0:T(8,128)(2,1)S(1)}, bf16[272,256]{1,0:T(8,128)(2,1)S(1)}, u32[]{:S(2)}, u32[]{:S(2)}) collective-permute-start(bf16[272,256]{1,0:T(8,128)(2,1)S(1)} %get-tuple-element.23), channel_id=1, source_target_pairs={{0,2},{2,0},{4,6},{6,4},{8,10},{10,8},{12,14},{14,12},{16,18},{18,... | collective-permute-start | bytes 417800 | tf_op jit(solution)/shard_map/ppermute | solution.py:246
  6.0 6.9 %collective-permute-start.3 = (bf16[272,256]{1,0:T(8,128)(2,1)S(1)}, bf16[272,256]{1,0:T(8,128)(2,1)S(1)}, u32[]{:S(2)}, u32[]{:S(2)}) collective-permute-start(bf16[272,256]{1,0:T(8,128)(2,1)S(1)} %add_convert_fusion), channel_id=1, source_target_pairs={{0,4},{2,6},{4,0},{6,2},{8,12},{10,14},{12,8},{14,10},{16,20},{18,... | collective-permute-start | bytes 417800 | tf_op jit(solution)/shard_map/ppermute | solution.py:246
  11.1 1.9 %collective-permute-start.2 = (bf16[272,256]{1,0:T(8,128)(2,1)S(1)}, bf16[272,256]{1,0:T(8,128)(2,1)S(1)}, u32[]{:S(2)}, u32[]{:S(2)}) collective-permute-start(bf16[272,256]{1,0:T(8,128)(2,1)S(1)} %get-tuple-element.28), channel_id=1, source_target_pairs={{0,2},{2,0},{4,6},{6,4},{8,10},{10,8},{12,14},{14,12},{16,18},{18,... | collective-permute-start | bytes 417800 | tf_op jit(solution)/shard_map/ppermute | solution.py:246
  11.4 1.2 %collective-permute-start.1 = (bf16[2,32,128]{2,1,0:T(8,128)(2,1)S(1)}, bf16[2,32,128]{2,1,0:T(8,128)(2,1)S(1)}, u32[]{:S(2)}, u32[]{:S(2)}) collective-permute-start(bf16[2,32,128]{2,1,0:T(8,128)(2,1)S(1)} %copy-done.4), channel_id=1, source_target_pairs={{0,2},{2,0},{4,6},{6,4},{8,10},{10,8},{12,14},{14,12},{16,18},{18,... | collective-permute-start | bytes 49160 | tf_op jit(solution)/shard_map/ppermute | solution.py:246
  13.0 5.6 %collective-permute-start.5 = (bf16[264,256]{1,0:T(8,128)(2,1)S(1)}, bf16[264,256]{1,0:T(8,128)(2,1)S(1)}, u32[]{:S(2)}, u32[]{:S(2)}) collective-permute-start(bf16[264,256]{1,0:T(8,128)(2,1)S(1)} %add_convert_fusion.2), channel_id=1, source_target_pairs={{0,8},{2,10},{4,12},{6,14},{8,0},{10,2},{12,4},{14,6},{16,24},{18,... | collective-permute-start | bytes 405512 | tf_op jit(solution)/shard_map/ppermute | solution.py:246
  14.9 3.7 %collective-permute-start.4 = (bf16[2,32,128]{2,1,0:T(8,128)(2,1)S(1)}, bf16[2,32,128]{2,1,0:T(8,128)(2,1)S(1)}, u32[]{:S(2)}, u32[]{:S(2)}) collective-permute-start(bf16[2,32,128]{2,1,0:T(8,128)(2,1)S(1)} %get-tuple-element.38), channel_id=1, source_target_pairs={{0,1},{1,0},{2,3},{3,2},{4,5},{5,4},{6,7},{7,6},{8,9},{9,8},{10,11... | collective-permute-start | bytes 49160 | tf_op jit(solution)/shard_map/ppermute | solution.py:246
  18.7 8.3 %collective-permute-start.6 = (bf16[264,256]{1,0:T(8,128)(2,1)S(1)}, bf16[264,256]{1,0:T(8,128)(2,1)S(1)}, u32[]{:S(2)}, u32[]{:S(2)}) collective-permute-start(bf16[264,256]{1,0:T(8,128)(2,1)S(1)} %add_convert_fusion.1.own_ref), channel_id=1, source_target_pairs={{0,16},{2,18},{4,20},{6,22},{8,24},{10,26},{12,28},{14,30},{16,0},... | collective-permute-start | bytes 405512 | tf_op jit(solution)/shard_map/ppermute | solution.py:246
  21.4 5.6 %collective-permute-start.7 = (bf16[128,128]{1,0:T(8,128)(2,1)S(1)}, bf16[128,128]{1,0:T(8,128)(2,1)S(1)}, u32[]{:S(2)}, u32[]{:S(2)}) collective-permute-start(bf16[128,128]{1,0:T(8,128)(2,1)S(1)} %bitcast.12), channel_id=1, source_target_pairs={{0,4},{2,6},{4,0},{6,2},{8,12},{10,14},{12,8},{14,10},{16,20},{18,... | collective-permute-start | bytes 98312 | tf_op jit(solution)/shard_map/ppermute | solution.py:246

commit v7 on v6

--- a/solution.py
+++ b/solution.py
@@ -270,7 +270,7 @@
         step *= 2
         own = (own.astype(F32) + got.astype(F32)).astype(BF)
         asked, candidates_late, own = lax.optimization_barrier((asked, candidates, own))
-        got = swap(own, step)
+        got = swap(own, step + step // 2)
     width = candidates.shape[2]
     rows = candidates_late.reshape(-1, width)
     base = jnp.dot(rows, w_hidden[:width], preferred_element_type=F32) + b_hidden

time: 37.1 us -> 36.5 us (0.984)
  waiting for transfers between devices: 7.47 us -> 5.79 us
  starting transfers between devices: 11.2 us -> 12.1 us
    ppermute x8, waiting for transfers between devices: 7.47 us -> 5.79 us  [swap(): return lax.ppermute(value, axis, [(i, i ^ step) for i in range(count)])]
    ppermute x8, starting transfers between devices: 11.2 us -> 12.1 us  [swap(): return lax.ppermute(value, axis, [(i, i ^ step) for i in range(count)])]
  transfers between devices with their start and end apart: 8 -> 8, of which waited for: 4 -> 5; matrix products, arithmetic and copies ran while one was open for 0% -> 0% of each run, Pallas kernels for 10% -> 11%
where the time goes in v7:
time: 36.5 us; the launch traced here: 36.3 us
  starting transfers between devices  12.1 us (33%)
  Pallas kernels  8.85 us (24%)
  blocking collectives  8.48 us (23%)
  waiting for transfers between devices  5.79 us (16%)
  between operations  0.77 us (2%)
    ppermute x8, starting transfers between devices, swap(): return lax.ppermute(value, axis, [(i, i ^ step) for i in range(count)])  12.1 us
    all_to_all x1, blocking collectives, on_device(): lax.all_to_all(partial, ('seq', 'cand'), 0, 0, tiled=True, axis_index_gro...  8.48 us
    ppermute x8, waiting for transfers between devices, swap(): return lax.ppermute(value, axis, [(i, i ^ step) for i in range(count)])  5.79 us
    pallas_call x2, Pallas kernels, pool_next(): pl.pallas_call(functools.partial(next_kernel, low, *plan, min(NEXT_BLOCK,...  3.83 us
    pallas_call x1, Pallas kernels, pool_first(): pl.pallas_call(functools.partial(first_kernel, low, *plan), grid=(slots /...  3.39 us
    pallas_call x1, Pallas kernels, rank(): pl.pallas_call(functools.partial(rank_kernel, users), out_shape=jax.Shape...  0.98 us
  transfers between devices with their start and end apart: 8, of which 5 were waited for; matrix products, arithmetic and copies ran while one was open for 0% of the time, Pallas kernels for 11%

profile of v7, /device:TPU:0, one launch (start us, length us, event | category | flops | bytes accessed | tf_op | source)
XLA Modules:
  0.0 36.3 jit_solution(2182719587093144942)
XLA Ops:
  0.7 3.4 %pool_first.1 = (bf16[272,256]{1,0:T(8,128)(2,1)S(1)}, bf16[128,8192]{1,0:T(8,128)(2,1)S(1)}, s32[1,8192]{1,0:T(1,128)S(1)}) custom-call(s32[1,1]{1,0:T(1,128)S(6)} %copy.10.live_ref, s32[1,8192]{1,0:T(1,128)} %ids_ref.1, f32[8192,128]{1,0:T(8,128)} %bitcast.15), custom_call_target="tpu_custom_call" | custom-call | tf_op jit(solution)/shard_map/pool_first/pallas_call | solution.py:113
  4.1 0.0 copy-start
  4.1 0.0 copy-start.5
  4.1 0.0 copy-start.1
  4.1 0.0 copy-start.2
  4.1 0.0 copy-start.3
  4.1 0.5 %collective-permute-start = (bf16[272,256]{1,0:T(8,128)(2,1)S(1)}, bf16[272,256]{1,0:T(8,128)(2,1)S(1)}, u32[]{:S(2)}, u32[]{:S(2)}) collective-permute-start(bf16[272,256]{1,0:T(8,128)(2,1)S(1)} %get-tuple-element.23), channel_id=1, source_target_pairs={{0,2},{2,0},{4,6},{6,4},{8,10},{10,8},{12,14},{14,12},{16,18},{18,... | collective-permute-start | bytes 417800 | tf_op jit(solution)/shard_map/ppermute | solution.py:246
  4.6 1.4 %pool_next.3 = f32[272,256]{1,0:T(8,128)S(1)} custom-call(s32[1,8192]{1,0:T(1,128)S(1)} %get-tuple-element.21.marked_ref, bf16[128,8192]{1,0:T(8,128)(2,1)S(1)} %get-tuple-element.24.turned_ref), custom_call_target="tpu_custom_call" | custom-call | tf_op jit(solution)/shard_map/pool_next/pallas_call | solution.py:142
  6.0 0.0 collective-permute-done
  6.0 2.6 %collective-permute-start.3 = (bf16[272,256]{1,0:T(8,128)(2,1)S(1)}, bf16[272,256]{1,0:T(8,128)(2,1)S(1)}, u32[]{:S(2)}, u32[]{:S(2)}) collective-permute-start(bf16[272,256]{1,0:T(8,128)(2,1)S(1)} %add_convert_fusion), channel_id=1, source_target_pairs={{0,4},{2,6},{4,0},{6,2},{8,12},{10,14},{12,8},{14,10},{16,20},{18,... | collective-permute-start | bytes 417800 | tf_op jit(solution)/shard_map/ppermute | solution.py:246
  8.6 2.5 %pool_next.2 = (f32[272,256]{1,0:T(8,128)S(1)}, bf16[272,256]{1,0:T(8,128)(2,1)S(1)}) custom-call(s32[1,8192]{1,0:T(1,128)S(1)} %get-tuple-element.21.marked_ref, bf16[128,8192]{1,0:T(8,128)(2,1)S(1)} %get-tuple-element.24.turned_ref), custom_call_target="tpu_custom_call" | custom-call | tf_op jit(solution)/shard_map/pool_next/pallas_call | solution.py:142
  11.1 0.3 collective-permute-start.2
  11.4 0.0 copy-done.4
  11.4 0.3 collective-permute-start.1
  11.7 0.9 %collective-permute-done.1 = bf16[2,32,128]{2,1,0:T(8,128)(2,1)S(1)} collective-permute-done((bf16[2,32,128]{2,1,0:T(8,128)(2,1)S(1)}, bf16[2,32,128]{2,1,0:T(8,128)(2,1)S(1)}, u32[]{:S(2)}, u32[]{:S(2)}) %collective-permute-start.1) | collective-permute-done | bytes 16416 | tf_op jit(solution)/shard_map/ppermute | solution.py:246
  12.6 0.4 %collective-permute-done.3 = bf16[272,256]{1,0:T(8,128)(2,1)S(1)} collective-permute-done((bf16[272,256]{1,0:T(8,128)(2,1)S(1)}, bf16[272,256]{1,0:T(8,128)(2,1)S(1)}, u32[]{:S(2)}, u32[]{:S(2)}) %collective-permute-start.3) | collective-permute-done | bytes 139296 | tf_op jit(solution)/shard_map/ppermute | solution.py:246
  13.0 0.0 collective-permute-done.2
  13.0 0.1 add_convert_fusion.2
  13.0 1.9 %collective-permute-start.5 = (bf16[264,256]{1,0:T(8,128)(2,1)S(1)}, bf16[264,256]{1,0:T(8,128)(2,1)S(1)}, u32[]{:S(2)}, u32[]{:S(2)}) collective-permute-start(bf16[264,256]{1,0:T(8,128)(2,1)S(1)} %add_convert_fusion.2), channel_id=1, source_target_pairs={{0,8},{2,10},{4,12},{6,14},{8,0},{10,2},{12,4},{14,6},{16,24},{18,... | collective-permute-start | bytes 405512 | tf_op jit(solution)/shard_map/ppermute | solution.py:246
  14.9 1.5 %collective-permute-start.4 = (bf16[2,32,128]{2,1,0:T(8,128)(2,1)S(1)}, bf16[2,32,128]{2,1,0:T(8,128)(2,1)S(1)}, u32[]{:S(2)}, u32[]{:S(2)}) collective-permute-start(bf16[2,32,128]{2,1,0:T(8,128)(2,1)S(1)} %get-tuple-element.38), channel_id=1, source_target_pairs={{0,1},{1,0},{2,3},{3,2},{4,5},{5,4},{6,7},{7,6},{8,9},{9,8},{10,11... | collective-permute-start | bytes 49160 | tf_op jit(solution)/shard_map/ppermute | solution.py:246
  16.4 2.2 %collective-permute-done.4 = bf16[2,32,128]{2,1,0:T(8,128)(2,1)S(1)} collective-permute-done((bf16[2,32,128]{2,1,0:T(8,128)(2,1)S(1)}, bf16[2,32,128]{2,1,0:T(8,128)(2,1)S(1)}, u32[]{:S(2)}, u32[]{:S(2)}) %collective-permute-start.4) | collective-permute-done | bytes 16416 | tf_op jit(solution)/shard_map/ppermute | solution.py:246
  18.7 0.0 collective-permute-done.5
  18.7 3.5 %collective-permute-start.6 = (bf16[264,256]{1,0:T(8,128)(2,1)S(1)}, bf16[264,256]{1,0:T(8,128)(2,1)S(1)}, u32[]{:S(2)}, u32[]{:S(2)}) collective-permute-start(bf16[264,256]{1,0:T(8,128)(2,1)S(1)} %add_convert_fusion.1.own_ref), channel_id=1, source_target_pairs={{0,24},{2,26},{4,28},{6,30},{8,16},{10,18},{12,20},{14,22},{16,8},... | collective-permute-start | bytes 405512 | tf_op jit(solution)/shard_map/ppermute | solution.py:246
  22.2 1.5 %collective-permute-start.7 = (bf16[128,128]{1,0:T(8,128)(2,1)S(1)}, bf16[128,128]{1,0:T(8,128)(2,1)S(1)}, u32[]{:S(2)}, u32[]{:S(2)}) collective-permute-start(bf16[128,128]{1,0:T(8,128)(2,1)S(1)} %bitcast.12), channel_id=1, source_target_pairs={{0,4},{2,6},{4,0},{6,2},{8,12},{10,14},{12,8},{14,10},{16,20},{18,... | collective-permute-start | bytes 98312 | tf_op jit(solution)/shard_map/ppermute | solution.py:246
  23.7 0.0 copy-done
  23.7 0.1 convolution_add_fusion.base_ref
  23.9 1.8 %collective-permute-done.6.got_ref = bf16[264,256]{1,0:T(8,128)(2,1)S(1)} collective-permute-done((bf16[264,256]{1,0:T(8,128)(2,1)S(1)}, bf16[264,256]{1,0:T(8,128)(2,1)S(1)}, u32[]{:S(2)}, u32[]{:S(2)}) %collective-permute-start.6) | collective-permute-done | bytes 135200 | tf_op jit(solution)/shard_map/ppermute | solution.py:246
  25.7 0.5 %collective-permute-done.7.other_ref = bf16[128,128]{1,0:T(8,128)(2,1)S(1)} collective-permute-done((bf16[128,128]{1,0:T(8,128)(2,1)S(1)}, bf16[128,128]{1,0:T(8,128)(2,1)S(1)}, u32[]{:S(2)}, u32[]{:S(2)}) %collective-permute-start.7) | collective-permute-done | bytes 32800 | tf_op jit(solution)/shard_map/ppermute | solution.py:246
  26.2 0.0 copy-done.2
  26.2 0.6 %attend.1 = bf16[8,32,256]{2,1,0:T(8,128)(2,1)S(1)} custom-call(bf16[264,256]{1,0:T(8,128)(2,1)S(1)} %add_convert_fusion.1.own_ref, bf16[264,256]{1,0:T(8,128)(2,1)S(1)} %collective-permute-done.6.got_ref, bf16[128,128]{1,0:T(8,128)(2,1)S(1)} %bitcast.13, bf16[128,128]{1,0:T(8,128)(2,1)S(1)} %collective-permute-done.7.other_ref, ...), custom_call_target="tpu_custom_call" | custom-call | tf_op jit(solution)/shard_map/attend/pallas_call | solution.py:196
  26.8 8.5 %all_to_all.5.got_ref = bf16[8,32,256]{2,1,0:T(8,128)(2,1)S(1)} all-to-all(bf16[8,32,256]{2,1,0:T(8,128)(2,1)S(1)} %attend.1), channel_id=1, replica_groups={{0,1,2,3,4,5,6,7},{8,9,10,11,12,13,14,15},{16,17,18,19,20,21,22,23},{24..., dimensions={0} | all-to-all | bytes 262144 | tf_op jit(solution)/shard_map/all_to_all | solution.py:281
  35.3 1.0 %rank.1 = f32[2,32]{1,0:T(2,128)} custom-call(bf16[8,32,256]{2,1,0:T(8,128)(2,1)S(1)} %all_to_all.5.got_ref, f32[64,512]{1,0:T(8,128)S(1)} %convolution_add_fusion.base_ref, bf16[256,512]{1,0:T(8,128)(2,1)S(1)} %copy-done, f32[1,512]{1,0:T(1,128)S(1)} %bitcast.14), custom_call_target="tpu_custom_call" | custom-call | tf_op jit(solution)/shard_map/rank/pallas_call | solution.py:232
  (9 shorter events, 0.1 us)
Async XLA Ops:
  0.7 10.7 %copy-start.4 = (bf16[2,32,128]{2,1,0:T(8,128)(2,1)S(1)}, bf16[2,32,128]{2,1,0:T(8,128)(2,1)}, u32[]{:S(2)}) copy-start(bf16[2,32,128]{2,1,0:T(8,128)(2,1)} %param.12) | copy-start | bytes 49156
  4.1 19.7 %copy-start = (bf16[256,512]{1,0:T(8,128)(2,1)S(1)}, bf16[256,512]{1,0:T(8,128)(2,1)}, u32[]{:S(2)}) copy-start(bf16[256,512]{1,0:T(8,128)(2,1)} %wh_ref.1) | copy-start | bytes 786436
  4.1 19.7 %copy-start.5 = (f32[512]{0:T(512)S(1)}, f32[512]{0:T(512)}, u32[]{:S(2)}) copy-start(f32[512]{0:T(512)} %param.16) | copy-start | bytes 6148
  4.1 22.1 %copy-start.1 = (bf16[128,128]{1,0:T(8,128)(2,1)S(1)}, bf16[128,128]{1,0:T(8,128)(2,1)}, u32[]{:S(2)}) copy-start(bf16[128,128]{1,0:T(8,128)(2,1)} %wq_ref.1) | copy-start | bytes 98308
  4.1 22.1 %copy-start.2 = (bf16[128,128]{1,0:T(8,128)(2,1)S(1)}, bf16[128,128]{1,0:T(8,128)(2,1)}, u32[]{:S(2)}) copy-start(bf16[128,128]{1,0:T(8,128)(2,1)} %wk_ref.1) | copy-start | bytes 98308
  4.1 31.2 %copy-start.3 = (f32[512]{0:T(512)S(1)}, f32[512]{0:T(512)}, u32[]{:S(2)}) copy-start(f32[512]{0:T(512)} %param.17) | copy-start | bytes 6148
  4.1 1.9 %collective-permute-start = (bf16[272,256]{1,0:T(8,128)(2,1)S(1)}, bf16[272,256]{1,0:T(8,128)(2,1)S(1)}, u32[]{:S(2)}, u32[]{:S(2)}) collective-permute-start(bf16[272,256]{1,0:T(8,128)(2,1)S(1)} %get-tuple-element.23), channel_id=1, source_target_pairs={{0,2},{2,0},{4,6},{6,4},{8,10},{10,8},{12,14},{14,12},{16,18},{18,... | collective-permute-start | bytes 417800 | tf_op jit(solution)/shard_map/ppermute | solution.py:246
  6.0 6.9 %collective-permute-start.3 = (bf16[272,256]{1,0:T(8,128)(2,1)S(1)}, bf16[272,256]{1,0:T(8,128)(2,1)S(1)}, u32[]{:S(2)}, u32[]{:S(2)}) collective-permute-start(bf16[272,256]{1,0:T(8,128)(2,1)S(1)} %add_convert_fusion), channel_id=1, source_target_pairs={{0,4},{2,6},{4,0},{6,2},{8,12},{10,14},{12,8},{14,10},{16,20},{18,... | collective-permute-start | bytes 417800 | tf_op jit(solution)/shard_map/ppermute | solution.py:246
  11.1 1.9 %collective-permute-start.2 = (bf16[272,256]{1,0:T(8,128)(2,1)S(1)}, bf16[272,256]{1,0:T(8,128)(2,1)S(1)}, u32[]{:S(2)}, u32[]{:S(2)}) collective-permute-start(bf16[272,256]{1,0:T(8,128)(2,1)S(1)} %get-tuple-element.28), channel_id=1, source_target_pairs={{0,2},{2,0},{4,6},{6,4},{8,10},{10,8},{12,14},{14,12},{16,18},{18,... | collective-permute-start | bytes 417800 | tf_op jit(solution)/shard_map/ppermute | solution.py:246
  11.4 1.2 %collective-permute-start.1 = (bf16[2,32,128]{2,1,0:T(8,128)(2,1)S(1)}, bf16[2,32,128]{2,1,0:T(8,128)(2,1)S(1)}, u32[]{:S(2)}, u32[]{:S(2)}) collective-permute-start(bf16[2,32,128]{2,1,0:T(8,128)(2,1)S(1)} %copy-done.4), channel_id=1, source_target_pairs={{0,2},{2,0},{4,6},{6,4},{8,10},{10,8},{12,14},{14,12},{16,18},{18,... | collective-permute-start | bytes 49160 | tf_op jit(solution)/shard_map/ppermute | solution.py:246
  13.0 5.6 %collective-permute-start.5 = (bf16[264,256]{1,0:T(8,128)(2,1)S(1)}, bf16[264,256]{1,0:T(8,128)(2,1)S(1)}, u32[]{:S(2)}, u32[]{:S(2)}) collective-permute-start(bf16[264,256]{1,0:T(8,128)(2,1)S(1)} %add_convert_fusion.2), channel_id=1, source_target_pairs={{0,8},{2,10},{4,12},{6,14},{8,0},{10,2},{12,4},{14,6},{16,24},{18,... | collective-permute-start | bytes 405512 | tf_op jit(solution)/shard_map/ppermute | solution.py:246
  14.9 3.7 %collective-permute-start.4 = (bf16[2,32,128]{2,1,0:T(8,128)(2,1)S(1)}, bf16[2,32,128]{2,1,0:T(8,128)(2,1)S(1)}, u32[]{:S(2)}, u32[]{:S(2)}) collective-permute-start(bf16[2,32,128]{2,1,0:T(8,128)(2,1)S(1)} %get-tuple-element.38), channel_id=1, source_target_pairs={{0,1},{1,0},{2,3},{3,2},{4,5},{5,4},{6,7},{7,6},{8,9},{9,8},{10,11... | collective-permute-start | bytes 49160 | tf_op jit(solution)/shard_map/ppermute | solution.py:246
  18.7 7.0 %collective-permute-start.6 = (bf16[264,256]{1,0:T(8,128)(2,1)S(1)}, bf16[264,256]{1,0:T(8,128)(2,1)S(1)}, u32[]{:S(2)}, u32[]{:S(2)}) collective-permute-start(bf16[264,256]{1,0:T(8,128)(2,1)S(1)} %add_convert_fusion.1.own_ref), channel_id=1, source_target_pairs={{0,24},{2,26},{4,28},{6,30},{8,16},{10,18},{12,20},{14,22},{16,8},... | collective-permute-start | bytes 405512 | tf_op jit(solution)/shard_map/ppermute | solution.py:246
  22.2 3.9 %collective-permute-start.7 = (bf16[128,128]{1,0:T(8,128)(2,1)S(1)}, bf16[128,128]{1,0:T(8,128)(2,1)S(1)}, u32[]{:S(2)}, u32[]{:S(2)}) collective-permute-start(bf16[128,128]{1,0:T(8,128)(2,1)S(1)} %bitcast.12), channel_id=1, source_target_pairs={{0,4},{2,6},{4,0},{6,2},{8,12},{10,14},{12,8},{14,10},{16,20},{18,... | collective-permute-start | bytes 98312 | tf_op jit(solution)/shard_map/ppermute | solution.py:246
